TPU v7x, 32 devices: a whole 2x2x4 slice. The times are simulated.
32 devices in a mesh: ops: 8 (over y, x, core), sec: 4 (over z).
Axes of the slice: x: 2, y: 2, z: 4, core: 2. Of those that a mesh axis runs over, the one named last changes fastest.
Arguments:
- psi: float32 [4, 512, 512], P('sec')
- left_ops: float32 [32, 4, 512, 512], P('ops', 'sec')
- right_ops: float32 [32, 4, 512, 512], P('ops', 'sec')
- links: int32 [32, 4], P('ops', 'sec'), may hold values from 0 to 4, as said below
Outputs:
- sigma: float32 [4, 512, 512], P('sec', 'ops')
- direction: float32 [4, 512, 512], P('sec', 'ops')
- energies: float32 [2], replicated
Inputs may be any that keep to these rules, and one draw needn't show every extreme that they name: `links`: A value of 4 means that the term has no block on that source sector.
All inputs are finite; a program needn't handle non-finite values.
Results may differ from a plain program's by a relative error of at most 0.0003.
Values sent between devices are 32-bit elements; how exact they have to be, the bound alone decides.
No kernel may reach another device: no remote copies, remote signals or barrier semaphores. Data moves between devices by JAX's collectives and lax.ppermute only.
A program may use at most 64 MiB of HBM per device.

v0:
```python
import jax
import jax.numpy as jnp
from jax import lax
from jax.sharding import PartitionSpec as P


def local(psi, left_ops, right_ops, links):
    highest = lax.Precision.HIGHEST
    sec_count, states, _ = psi.shape
    term_count = left_ops.shape[0]
    ops_width = lax.axis_size("ops")
    sec_width = lax.axis_size("sec")
    sectors = sec_count * sec_width
    row_count = states // ops_width
    pair_count = term_count * sec_count
    lefts = left_ops.reshape(pair_count, states, states)
    right_blocks = right_ops.reshape(pair_count, states, states)
    targets = links.reshape(pair_count)

    def contribute(which):

        def working(unused):
            product_left = jnp.dot(
                lefts[which],
                psi[which % sec_count],
                precision=highest,
                preferred_element_type=jnp.float32,
            )
            return jnp.dot(
                product_left,
                right_blocks[which].T,
                precision=highest,
                preferred_element_type=jnp.float32,
            )

        def resting(unused):
            return jnp.zeros((states, states), jnp.float32)

        return lax.cond(targets[which] < sectors, working, resting, 0)

    contributions = lax.map(contribute, jnp.arange(pair_count))
    sector_extent = jnp.arange(sectors, dtype=jnp.int32)
    selector = (targets[None, :] == sector_extent[:, None]).astype(jnp.float32)
    sector_sigma = lax.psum_scatter(
        jnp.einsum("dk,kxn->dxn", selector, contributions, precision=highest),
        "sec",
        scatter_dimension=0,
        tiled=True,
    )
    sigma = lax.psum_scatter(sector_sigma, "ops", scatter_dimension=1, tiled=True)
    psi_rows = lax.dynamic_slice_in_dim(psi, lax.axis_index("ops") * row_count, row_count, 1)
    correlation_local = jnp.sum(psi_rows * sigma)
    weight_local = jnp.sum(psi_rows * psi_rows)
    correlation, weight = lax.psum((correlation_local, weight_local), ("ops", "sec"))
    theta = correlation / weight
    residual_vector = sigma - theta * psi_rows
    residual_squared = lax.psum(jnp.sum(residual_vector * residual_vector), ("ops", "sec"))
    norm_scale_factor = jnp.sqrt(residual_squared)
    direction = residual_vector / norm_scale_factor
    energies = jnp.stack([theta, norm_scale_factor])
    return (sigma, direction, energies)


def solution(mesh):
    return jax.shard_map(
        local,
        mesh=mesh,
        in_specs=(
            P("sec", None, None),
            P("ops", "sec", None, None),
            P("ops", "sec", None, None),
            P("ops", "sec"),
        ),
        out_specs=(P("sec", "ops", None), P("sec", "ops", None), P()),
        check_vma=False,
    )
```

profile of v0, /device:TPU:0, one launch (start us, length us, event | category | flops | bytes accessed | tf_op | source)
XLA Modules:
  0.0 387.9 jit_solution(18152413996534821973)
XLA Ops:
  7.2 131.1 %while.10 = (s32[]{:T(128)}, f32[4,512,512]{2,0,1:T(4,128)}, s32[4]{0:T(128)S(1)}, s32[4]{0:T(128)}, f32[4,512,512]{2,1,0:T(8,128)}, /*index=5*/f32[1,512,512]{2...) while((s32[]{:T(128)}, f32[4,512,512]{2,0,1:T(4,128)}, ...), condition=%wide.region_3.4_spmd, body=%wide.region_0.3_spmd.sunk | while | flops 3221225472 | bytes 10486027 | solution.py:41
  9.8 1.2 dynamic_slice.30
  11.8 1.1 copy.28
  12.9 20.9 %dynamic_update_slice.5 = f32[4,512,512]{2,0,1:T(4,128)} dynamic-update-slice(f32[4,512,512]{2,0,1:T(4,128)} %get-tuple-element.139, f32[1,512,512]{2,0,1:T(1,128)S(1)} %copy.28, s32[]{:T(128)} %get-tuple-element.138, s32[]{:T(128)} %constant.27.clone.1..sunk, s32[]{:T(128)} %constant.27.clone.1..sunk) | dynamic-update-slice | bytes 2097156 | tf_op jit(solution)/shard_map/while/body/jit(dynamic_update_index_in_dim)/dynamic_update_slice | solution.py:41
  36.3 1.2 dynamic_slice.30
  38.2 8.4 %conditional.2 = (f32[1,512,512]{2,1,0:T(8,128)S(1)}) conditional(s32[]{:T(128)} %bitcast.29, () %tuple.37, (s32[]{:T(128)}, f32[4,512,512]{2,1,0:T(8,128)}, f32[1,512,512]{2,1,0:T(8,128)}, f32[4,512,512]{2,1,0:T(8,128)}) %tuple.38), branch_computations={%region_1.1_spmd, %region_2.2_spmd} | conditional | flops 3221225472 | bytes 6291506 | solution.py:39
  40.2 3.4 fusion.1
  43.6 3.1 convolution_bitcast_fusion
  46.7 1.1 copy.28
  47.7 20.9 %dynamic_update_slice.5 = f32[4,512,512]{2,0,1:T(4,128)} dynamic-update-slice(f32[4,512,512]{2,0,1:T(4,128)} %get-tuple-element.139, f32[1,512,512]{2,0,1:T(1,128)S(1)} %copy.28, s32[]{:T(128)} %get-tuple-element.138, s32[]{:T(128)} %constant.27.clone.1..sunk, s32[]{:T(128)} %constant.27.clone.1..sunk) | dynamic-update-slice | bytes 2097156 | tf_op jit(solution)/shard_map/while/body/jit(dynamic_update_index_in_dim)/dynamic_update_slice | solution.py:41
  71.2 1.2 dynamic_slice.30
  73.1 8.4 %conditional.2 = (f32[1,512,512]{2,1,0:T(8,128)S(1)}) conditional(s32[]{:T(128)} %bitcast.29, () %tuple.37, (s32[]{:T(128)}, f32[4,512,512]{2,1,0:T(8,128)}, f32[1,512,512]{2,1,0:T(8,128)}, f32[4,512,512]{2,1,0:T(8,128)}) %tuple.38), branch_computations={%region_1.1_spmd, %region_2.2_spmd} | conditional | flops 3221225472 | bytes 6291506 | solution.py:39
  75.0 3.4 fusion.1
  78.4 3.1 convolution_bitcast_fusion
  81.5 1.1 copy.28
  82.6 20.9 %dynamic_update_slice.5 = f32[4,512,512]{2,0,1:T(4,128)} dynamic-update-slice(f32[4,512,512]{2,0,1:T(4,128)} %get-tuple-element.139, f32[1,512,512]{2,0,1:T(1,128)S(1)} %copy.28, s32[]{:T(128)} %get-tuple-element.138, s32[]{:T(128)} %constant.27.clone.1..sunk, s32[]{:T(128)} %constant.27.clone.1..sunk) | dynamic-update-slice | bytes 2097156 | tf_op jit(solution)/shard_map/while/body/jit(dynamic_update_index_in_dim)/dynamic_update_slice | solution.py:41
  106.0 1.2 dynamic_slice.30
  107.9 8.4 %conditional.2 = (f32[1,512,512]{2,1,0:T(8,128)S(1)}) conditional(s32[]{:T(128)} %bitcast.29, () %tuple.37, (s32[]{:T(128)}, f32[4,512,512]{2,1,0:T(8,128)}, f32[1,512,512]{2,1,0:T(8,128)}, f32[4,512,512]{2,1,0:T(8,128)}) %tuple.38), branch_computations={%region_1.1_spmd, %region_2.2_spmd} | conditional | flops 3221225472 | bytes 6291506 | solution.py:39
  109.9 3.4 fusion.1
  113.3 3.1 convolution_bitcast_fusion
  116.3 1.1 copy.28
  117.4 20.9 %dynamic_update_slice.5 = f32[4,512,512]{2,0,1:T(4,128)} dynamic-update-slice(f32[4,512,512]{2,0,1:T(4,128)} %get-tuple-element.139, f32[1,512,512]{2,0,1:T(1,128)S(1)} %copy.28, s32[]{:T(128)} %get-tuple-element.138, s32[]{:T(128)} %constant.27.clone.1..sunk, s32[]{:T(128)} %constant.27.clone.1..sunk) | dynamic-update-slice | bytes 2097156 | tf_op jit(solution)/shard_map/while/body/jit(dynamic_update_index_in_dim)/dynamic_update_slice | solution.py:41
  138.3 6.2 %fusion.9 = f32[4,512,512]{2,0,1:T(4,128)S(1)} fusion(f32[4,512,512]{2,0,1:T(4,128)} %get-tuple-element.56, s32[4]{0:T(128)} %get-tuple-element.170), kind=kOutput, calls=%fused_computation.16 | convolution fusion | flops 50331664 | bytes 8388624 | tf_op jit(solution)/shard_map/dk,kxn->dxn/dot_general | solution.py:45
  144.6 3.2 copy.12
  148.0 85.8 %reduce-scatter.2.cloned.1.call-done = f32[1,512,512]{2,1,0:T(8,128)} async-done(((f32[4,512,512]{2,1,0:T(8,128)}), f32[1,512,512]{2,1,0:T(8,128)}) %reduce-scatter.2.cloned.1.call-update) | async-done | bytes 1048592 | tf_op jit(solution)/shard_map/reduce_scatter | solution.py:44
  233.8 3.3 copy.13
  238.4 0.9 constant_dynamic-slice_fusion.1
  239.3 55.2 %all-reduce.4.cloned.1.call-done = f32[1,512,512]{2,0,1:T(1,128)} async-done(((f32[1,512,512]{2,0,1:T(1,128)}), f32[1,512,512]{2,0,1:T(1,128)}) %all-reduce.4.cloned.1.call-update) | async-done | bytes 1048592
  294.5 1.8 multiply_reduce_fusion.1
  296.9 39.4 %all-reduce.1 = (f32[]{:T(128)}, f32[]{:T(128)}) all-reduce(f32[]{:T(128)} %get-tuple-element.64, f32[]{:T(128)} %get-tuple-element.63), channel_id=1, replica_groups=mesh['ops'=8,'sec'=4] {'ops','sec'}, use_global_device_ids=true, to_apply=%region_7.8 | all-reduce | flops 2 | bytes 16 | tf_op jit(solution)/shard_map/psum | solution.py:54
  337.7 0.9 multiply_reduce_fusion
  338.6 40.5 %psum.23 = f32[]{:T(128)} all-reduce(f32[]{:T(128)} %get-tuple-element.81), channel_id=1, replica_groups=mesh['ops'=8,'sec'=4] {'ops','sec'}, use_global_device_ids=true, to_apply=%region_11.12 | all-reduce | flops 1 | bytes 8 | tf_op jit(solution)/shard_map/psum | solution.py:57
  (19 shorter events, 5.4 us)
Async XLA Ops:
  7.2 226.7 %reduce-scatter.2.cloned.1.call-start = ((), (), s32[]{:S(2)}) async-start(), calls=%async_computation.1 | async-start | bytes 5242880 | tf_op jit(solution)/shard_map/reduce_scatter | solution.py:44
  147.8 89.4 %copy-start = (u32[32]{0:T(128)S(1)}, u32[32]{0:T(128)}, u32[]{:S(2)}) copy-start(u32[32]{0:T(128)} %constant.47) | copy-start | bytes 388
  147.8 146.7 %all-reduce.4.cloned.1.call-start = ((), (), s32[]{:S(2)}) async-start(), calls=%async_computation.2 | async-start | bytes 2097152
Sparse Core Ops, SparseCore 0:
  147.9 85.8 reduce-scatter.1
  237.3 57.1 all-reduce.3
where the time goes:
time: 391 us; the launch traced here: 388 us
  waiting for transfers between devices  141 us (36%)
  local copies, waits for them, and re-layouts  105 us (27%)
  blocking collectives  79.9 us (20%)
  matrix products  25.6 us (7%)
  between operations  16.8 us (4%)
  loops' own time  16.4 us (4%)
    dynamic_update_slice x8, local copies, waits for them, and re-layouts, local(): contributions = lax.map(contribute, jnp.arange(pair_count))  87.9 us
    reduce_scatter x1, waiting for transfers between devices, local(): lax.psum_scatter(jnp.einsum('dk,kxn->dxn', selector, contributions, preci...  85.8 us
    unnamed x3, waiting for transfers between devices  55.2 us
    psum x1, blocking collectives, local(): lax.psum(jnp.sum(residual_vector * residual_vector), ('ops', 'sec'))  40.5 us
    psum x1, blocking collectives, local(): lax.psum((correlation_local, weight_local), ('ops', 'sec'))  39.4 us
    another operation x1, loops' own time, local(): contributions = lax.map(contribute, jnp.arange(pair_count))  10.5 us
    dot_general x3, matrix products, working(): jnp.dot(lefts[which], psi[which % sec_count], precision=highest, preferre...  10.1 us
    dot_general x3, matrix products, working(): jnp.dot(product_left, right_blocks[which].T, precision=highest, preferred...  9.25 us
  transfers between devices with their start and end apart: 2, of which 2 were waited for; matrix products, arithmetic and copies ran while one was open for 0% of the time, Pallas kernels for 0%

commit v1 on v0

v1 whole, which is shorter than its diff:
```python
import functools

import jax
import jax.numpy as jnp
from jax import lax
from jax.experimental import pallas as pl
from jax.experimental.pallas import tpu as pltpu
from jax.sharding import PartitionSpec as P

PIECES = (32, 32)

NT = (((1,), (1,)), ((), ()))
NN = (((1,), (0,)), ((), ()))


def log2(n):
    bits = n.bit_length() - 1
    assert n == 1 << bits
    return bits


def bit_orders(bits):
    first = list(range(1, bits))
    turn = (bits - 1) // 2
    return first, first[turn:] + first[:turn]


def split(x):
    high = x.astype(jnp.bfloat16)
    low = (x - high.astype(jnp.float32)).astype(jnp.bfloat16)
    return high, low


def dot3(a, b_high, b_low, dims):
    a_high, a_low = split(a)
    rows = a.shape[0]
    both = lax.dot_general(
        jnp.concatenate([a_high, a_low], 0), b_high, dims, preferred_element_type=jnp.float32
    )
    cross = lax.dot_general(a_high, b_low, dims, preferred_element_type=jnp.float32)
    return both[:rows] + (both[rows:] + cross)


def sigma_kernel(orders, ops_bits, sectors, links_ref, psi_ref, left_ref, right_ref, keep_ref, send_ref, psi_high, psi_low):
    pair = pl.program_id(0)
    rows, states = left_ref.shape[2:]
    slots = 1 << (ops_bits - 1)
    me = lax.axis_index("ops")
    core = me & 1

    @pl.when(pair == 0)
    def _():
        keep_ref[...] = jnp.zeros_like(keep_ref)
        send_ref[...] = jnp.zeros_like(send_ref)
        high, low = split(psi_ref[0])
        psi_high[...] = high
        psi_low[...] = low

    target = links_ref[pair, 0]

    @pl.when(target < sectors)
    def _():
        slot = target ^ lax.axis_index("sec")
        blocks = []
        for away in range(2):
            owner_core = core ^ away
            for q in range(slots):
                masks = [
                    sum(1 << order[step] for step in range(ops_bits - 1) if (q >> (ops_bits - 2 - step)) & 1)
                    for order in orders
                ]
                block = me ^ away ^ jnp.where(owner_core == 0, masks[0], masks[1])
                blocks.append(left_ref[0, block])
        product_left = dot3(jnp.concatenate(blocks, 0), psi_high[...], psi_low[...], NN)
        right_high, right_low = split(right_ref[0])
        product = dot3(product_left, right_high, right_low, NT)
        product = product.reshape(2, slots, rows, states)
        for q in range(slots):
            keep_ref[q, slot] += product[0, q]
            send_ref[q, slot] += product[1, q]


def partial_sigma(psi, lefts, rights, links, piece, start, ops_bits, sectors):
    pairs, owners, rows, states = lefts.shape
    slots = owners // 2
    out = jax.ShapeDtypeStruct((slots, sectors, piece, states), jnp.float32)
    whole = pl.BlockSpec((slots, sectors, piece, states), lambda p: (0, 0, 0, 0))
    return pl.pallas_call(
        functools.partial(sigma_kernel, bit_orders(ops_bits), ops_bits, sectors),
        grid=(pairs,),
        in_specs=[
            pl.BlockSpec(memory_space=pltpu.SMEM),
            pl.BlockSpec((1, states, states), lambda p: (0, 0, 0)),
            pl.BlockSpec((1, owners, piece, states), lambda p: (p, 0, start // piece, 0)),
            pl.BlockSpec((1, states, states), lambda p: (p, 0, 0)),
        ],
        out_specs=[whole, whole],
        out_shape=[out, out],
        scratch_shapes=[pltpu.VMEM((states, states), jnp.bfloat16)] * 2,
        compiler_params=pltpu.CompilerParams(
            dimension_semantics=("arbitrary",), vmem_limit_bytes=48 * 2**20
        ),
        cost_estimate=pl.CostEstimate(
            flops=12 * pairs * owners * piece * states * states,
            bytes_accessed=4 * (pairs * states * states + owners * piece * states * (pairs + sectors)),
            transcendentals=0,
        ),
        name="partial_sigma",
    )(links, psi, lefts, rights)


def stats_kernel(psi_ref, sigma_ref, stats_ref):
    psi = psi_ref[0]
    sigma = sigma_ref[0]
    weight = jnp.sum(psi * psi)
    correlation = jnp.sum(psi * sigma)
    theta = jnp.where(weight > 0.0, correlation / weight, 0.0)
    residual = sigma - theta * psi
    squared = jnp.sum(residual * residual)
    lane = lax.broadcasted_iota(jnp.int32, stats_ref.shape, 1)
    stats_ref[...] = jnp.where(lane == 0, weight, jnp.where(lane == 1, theta, jnp.where(lane == 2, squared, 0.0)))


def finish_kernel(psi_ref, sigma_ref, stats_ref, direction_ref, energies_ref):
    weights = stats_ref[:, 0:1]
    thetas = stats_ref[:, 1:2]
    squares = stats_ref[:, 2:3]
    theta = jnp.sum(weights * thetas) / jnp.sum(weights)
    apart = thetas - theta
    norm = jnp.sqrt(jnp.sum(squares + weights * apart * apart))
    direction_ref[0] = (sigma_ref[0] - theta * psi_ref[0]) / norm
    lane = lax.broadcasted_iota(jnp.int32, energies_ref.shape, 1)
    energies_ref[...] = jnp.where(lane == 0, theta, norm)


def local(psi, left_ops, right_ops, links):
    ops_width = lax.axis_size("ops")
    sectors = lax.axis_size("sec")
    ops_bits = log2(ops_width)
    log2(sectors)
    pairs, _, states, _ = left_ops.shape
    rows = states // ops_width
    lefts = left_ops.reshape(pairs, ops_width, rows, states)
    rights = right_ops.reshape(pairs, states, states)
    orders = bit_orders(ops_bits)
    pieces = PIECES if sum(PIECES) == rows else (rows // 2, rows // 2)
    sigma_pieces = []
    start = 0
    for piece in pieces:
        keep, send = partial_sigma(psi, lefts, rights, links, piece, start, ops_bits, sectors)
        start += piece
        parts = [keep, lax.ppermute(send, "ops", [(i, i ^ 1) for i in range(ops_width)])]
        for step in range(ops_bits - 1):
            half = parts[0].shape[0] // 2
            partner = [(i, i ^ (1 << orders[i & 1][step])) for i in range(ops_width)]
            came = lax.ppermute(sum(p[half:] for p in parts), "ops", partner)
            parts = [p[:half] for p in parts] + [came]
        parts = [p[0] for p in parts]
        mine = sum(p[0] for p in parts)
        for q in range(1, sectors):
            mine = mine + lax.ppermute(sum(p[q] for p in parts), "sec", [(i, i ^ q) for i in range(sectors)])
        sigma_pieces.append(mine)
    sigma = jnp.concatenate(sigma_pieces, 0)[None]
    index = lax.axis_index("ops")
    psi_rows = lax.dynamic_slice_in_dim(psi, index * rows, rows, 1)
    devices = ops_width * sectors
    stats = pl.pallas_call(
        stats_kernel,
        out_shape=jax.ShapeDtypeStruct((devices, 128), jnp.float32),
        name="stats",
    )(psi_rows, sigma)
    stats = lax.all_to_all(stats, ("ops", "sec"), 0, 0, tiled=True)
    direction, energies = pl.pallas_call(
        finish_kernel,
        out_shape=[
            jax.ShapeDtypeStruct((1, rows, states), jnp.float32),
            jax.ShapeDtypeStruct((1, 128), jnp.float32),
        ],
        name="finish",
    )(psi_rows, sigma, stats)
    return (sigma, direction, energies[0, :2])


def solution(mesh):
    return jax.shard_map(
        local,
        mesh=mesh,
        in_specs=(
            P("sec", None, None),
            P("ops", "sec", None, None),
            P("ops", "sec", None, None),
            P("ops", "sec"),
        ),
        out_specs=(P("sec", "ops", None), P("sec", "ops", None), P()),
        check_vma=False,
    )
```

time: 391 us -> 72.7 us (0.19)
  waiting for transfers between devices: 141 us -> 12.3 us
  local copies, waits for them, and re-layouts: 105 us -> 4.72 us
  blocking collectives: 79.9 us -> 10.2 us
  matrix products: 25.6 us -> 0 us
  starting transfers between devices: 0.26 us -> 20.5 us
  loops' own time: 16.4 us -> 0 us
  between operations: 16.8 us -> 0.69 us
  Pallas kernels: 0 us -> 15.1 us
  other arithmetic: 3.27 us -> 8.43 us
    dynamic_update_slice x8 -> x0, local copies, waits for them, and re-layouts: 87.9 us -> none  [local(): contributions = lax.map(contribute, jnp.arange(pair_count))]
    reduce_scatter x1 -> x0, waiting for transfers between devices: 85.8 us -> none  [local(): lax.psum_scatter(jnp.einsum('dk,kxn->dxn', selector, contributions, preci...]
    psum x2 -> x0, blocking collectives: 79.9 us -> none  [the longest x1 40.5 us: local(): lax.psum(jnp.sum(residual_vector * residual_vector), ('ops', 'sec'))]
    unnamed x3 -> x0, waiting for transfers between devices: 55.2 us -> none
    dot_general x7 -> x0, matrix products: 25.6 us -> none  [the longest x3 10.1 us: working(): jnp.dot(lefts[which], psi[which % sec_count], precision=highest, preferre...]
    ppermute x0 -> x12, starting transfers between devices: none -> 20.5 us  [the longest x4 9.99 us: local(): came = lax.ppermute(sum((p[half:] for p in parts)), 'ops', partner)]
    another operation x5 -> x0, loops' own time: 16.4 us -> none  [the longest x1 10.5 us: local(): contributions = lax.map(contribute, jnp.arange(pair_count))]
    pallas_call x0 -> x4, Pallas kernels: none -> 15.1 us  [the longest x2 11 us: partial_sigma(): pl.pallas_call(functools.partial(sigma_kernel, bit_orders(ops_bits), ops_...]
  transfers between devices with their start and end apart: 2 -> 12, of which waited for: 2 -> 6; matrix products, arithmetic and copies ran while one was open for 0% -> 12% of each run, Pallas kernels for 0% -> 8%
where the time goes in v1:
time: 72.7 us; the launch traced here: 71.9 us
  starting transfers between devices  20.5 us (28%)
  Pallas kernels  15.1 us (21%)
  waiting for transfers between devices  12.3 us (17%)
  blocking collectives  10.2 us (14%)
  other arithmetic  8.43 us (12%)
  local copies, waits for them, and re-layouts  4.72 us (6%)
    pallas_call x2, Pallas kernels, partial_sigma(): pl.pallas_call(functools.partial(sigma_kernel, bit_orders(ops_bits), ops_...  11 us
    all_to_all x1, blocking collectives, local(): stats = lax.all_to_all(stats, ('ops', 'sec'), 0, 0, tiled=True)  10.2 us
    ppermute x4, starting transfers between devices, local(): came = lax.ppermute(sum((p[half:] for p in parts)), 'ops', partner)  9.99 us
    ppermute x4, waiting for transfers between devices, local(): came = lax.ppermute(sum((p[half:] for p in parts)), 'ops', partner)  8.58 us
    ppermute x6, starting transfers between devices, local(): lax.ppermute(sum((p[q] for p in parts)), 'sec', [(i, i ^ q) for i in rang...  8 us
    add x4, other arithmetic, local(): came = lax.ppermute(sum((p[half:] for p in parts)), 'ops', partner)  3.94 us
    ppermute x6, waiting for transfers between devices, local(): lax.ppermute(sum((p[q] for p in parts)), 'sec', [(i, i ^ q) for i in rang...  3.55 us
    ppermute x2, starting transfers between devices, local(): lax.ppermute(send, 'ops', [(i, i ^ 1) for i in range(ops_width)])  2.46 us
  transfers between devices with their start and end apart: 12, of which 6 were waited for; matrix products, arithmetic and copies ran while one was open for 12% of the time, Pallas kernels for 8%

profile of v1, /device:TPU:0, one launch (start us, length us, event | category | flops | bytes accessed | tf_op | source)
XLA Modules:
  0.0 71.9 jit_solution(3173625843194643165)
XLA Ops:
  0.6 0.7 %copy.9.links_ref = s32[4,1]{1,0:T(4,128)S(1)} copy(s32[4,1]{0,1:T(1,128)} %param.7) | data formatting | bytes 32 | tf_op args[3]
  1.4 1.2 %copy-done = f32[1,512,512]{2,1,0:T(8,128)S(1)} copy-done((f32[1,512,512]{2,1,0:T(8,128)S(1)}, f32[1,512,512]{2,1,0:T(8,128)}, u32[]{:S(2)}) %copy-start) | copy-done | bytes 1048600
  2.6 5.5 %partial_sigma.2 = (f32[4,4,32,512]{3,2,1,0:T(8,128)S(1)}, f32[4,4,32,512]{3,2,1,0:T(8,128)S(1)}) custom-call(s32[4,1]{1,0:T(4,128)S(1)} %copy.9.links_ref, f32[1,512,512]{2,1,0:T(8,128)S(1)} %copy-done, f32[4,8,64,512]{3,2,1,0:T(8,128)} %bitcast.40, f32[4,512,512]{2,1,0:T(8,128)} %bitcast.42), custom_call_target="tpu_custom_call" | custom-call | flops 3221225472 | bytes 8388608 | tf_op jit(solution)/shard_map/partial_sigma/pallas_call | solution.py:88
  8.1 1.4 %collective-permute-start = (f32[4,4,32,512]{3,2,1,0:T(8,128)S(1)}, f32[4,4,32,512]{3,2,1,0:T(8,128)S(1)}, u32[]{:S(2)}, u32[]{:S(2)}) collective-permute-start(f32[4,4,32,512]{3,2,1,0:T(8,128)S(1)} %get-tuple-element.10), channel_id=1, source_target_pairs={{0,4},{4,0},{8,12},{12,8},{16,20},{20,16},{24,28},{28,24},{1,5},{5... | collective-permute-start | bytes 3145736 | tf_op jit(solution)/shard_map/ppermute | solution.py:152
  9.5 5.5 %partial_sigma.3 = (f32[4,4,32,512]{3,2,1,0:T(8,128)S(1)}, f32[4,4,32,512]{3,2,1,0:T(8,128)S(1)}) custom-call(s32[4,1]{1,0:T(4,128)S(1)} %copy.9.links_ref, f32[1,512,512]{2,1,0:T(8,128)S(1)} %copy-done, f32[4,8,64,512]{3,2,1,0:T(8,128)} %bitcast.41, f32[4,512,512]{2,1,0:T(8,128)} %bitcast.43), custom_call_target="tpu_custom_call" | custom-call | flops 3221225472 | bytes 8388608 | tf_op jit(solution)/shard_map/partial_sigma/pallas_call | solution.py:88
  15.0 1.0 %collective-permute-start.6 = (f32[4,4,32,512]{3,2,1,0:T(8,128)S(1)}, f32[4,4,32,512]{3,2,1,0:T(8,128)S(1)}, u32[]{:S(2)}, u32[]{:S(2)}) collective-permute-start(f32[4,4,32,512]{3,2,1,0:T(8,128)S(1)} %get-tuple-element.12), channel_id=1, source_target_pairs={{0,4},{4,0},{8,12},{12,8},{16,20},{20,16},{24,28},{28,24},{1,5},{5... | collective-permute-start | bytes 3145736 | tf_op jit(solution)/shard_map/ppermute | solution.py:152
  16.0 1.0 %slice_add_fusion.1 = f32[2,4,32,512]{3,2,1,0:T(8,128)} fusion(f32[4,4,32,512]{3,2,1,0:T(8,128)S(1)} %collective-permute-done, f32[4,4,32,512]{3,2,1,0:T(8,128)S(1)} %get-tuple-element.9), kind=kLoop, calls=%fused_computation.1 | loop fusion | flops 131072 | bytes 1572864 | tf_op jit(solution)/shard_map/add | solution.py:156
  17.0 1.2 %collective-permute-start.1 = (f32[2,4,32,512]{3,2,1,0:T(8,128)}, f32[2,4,32,512]{3,2,1,0:T(8,128)}, u32[]{:S(2)}, u32[]{:S(2)}) collective-permute-start(f32[2,4,32,512]{3,2,1,0:T(8,128)} %slice_add_fusion.1), channel_id=1, source_target_pairs={{0,8},{4,20},{8,0},{12,28},{16,24},{20,4},{24,16},{28,12},{1,9},{5... | collective-permute-start | bytes 1572872 | tf_op jit(solution)/shard_map/ppermute | solution.py:156
  18.3 0.9 %slice_add_fusion = f32[2,4,32,512]{3,2,1,0:T(8,128)} fusion(f32[4,4,32,512]{3,2,1,0:T(8,128)S(1)} %collective-permute-done.6, f32[4,4,32,512]{3,2,1,0:T(8,128)S(1)} %get-tuple-element.11), kind=kLoop, calls=%fused_computation | loop fusion | flops 131072 | bytes 1572864 | tf_op jit(solution)/shard_map/add | solution.py:156
  19.2 1.5 %collective-permute-start.7 = (f32[2,4,32,512]{3,2,1,0:T(8,128)}, f32[2,4,32,512]{3,2,1,0:T(8,128)}, u32[]{:S(2)}, u32[]{:S(2)}) collective-permute-start(f32[2,4,32,512]{3,2,1,0:T(8,128)} %slice_add_fusion), channel_id=1, source_target_pairs={{0,8},{4,20},{8,0},{12,28},{16,24},{20,4},{24,16},{28,12},{1,9},{5... | collective-permute-start | bytes 1572872 | tf_op jit(solution)/shard_map/ppermute | solution.py:156
  20.7 5.8 %collective-permute-done.1 = f32[2,4,32,512]{3,2,1,0:T(8,128)} collective-permute-done((f32[2,4,32,512]{3,2,1,0:T(8,128)}, f32[2,4,32,512]{3,2,1,0:T(8,128)}, u32[]{:S(2)}, u32[]{:S(2)}) %collective-permute-start.1) | collective-permute-done | bytes 524320 | tf_op jit(solution)/shard_map/ppermute | solution.py:156
  26.5 1.1 %slice_add_fusion.4 = f32[1,4,32,512]{3,2,1,0:T(8,128)S(1)} fusion(f32[2,4,32,512]{3,2,1,0:T(8,128)} %collective-permute-done.1, f32[4,4,32,512]{3,2,1,0:T(8,128)} %copy-done.1, f32[4,4,32,512]{3,2,1,0:T(8,128)S(1)} %get-tuple-element.9), kind=kLoop, calls=%fused_computation.4 | loop fusion | flops 131072 | bytes 1048576 | tf_op jit(solution)/shard_map/add | solution.py:156
  27.6 3.1 %collective-permute-start.2 = (f32[1,4,32,512]{3,2,1,0:T(8,128)S(1)}, f32[1,4,32,512]{3,2,1,0:T(8,128)S(1)}, u32[]{:S(2)}, u32[]{:S(2)}) collective-permute-start(f32[1,4,32,512]{3,2,1,0:T(8,128)S(1)} %slice_add_fusion.4), channel_id=1, source_target_pairs={{0,16},{4,12},{8,24},{12,4},{16,0},{20,28},{24,8},{28,20},{1,17},{... | collective-permute-start | bytes 786440 | tf_op jit(solution)/shard_map/ppermute | solution.py:156
  30.7 2.8 %collective-permute-done.7 = f32[2,4,32,512]{3,2,1,0:T(8,128)} collective-permute-done((f32[2,4,32,512]{3,2,1,0:T(8,128)}, f32[2,4,32,512]{3,2,1,0:T(8,128)}, u32[]{:S(2)}, u32[]{:S(2)}) %collective-permute-start.7) | collective-permute-done | bytes 524320 | tf_op jit(solution)/shard_map/ppermute | solution.py:156
  33.4 1.0 %slice_add_fusion.2 = f32[1,4,32,512]{3,2,1,0:T(8,128)S(1)} fusion(f32[2,4,32,512]{3,2,1,0:T(8,128)} %collective-permute-done.7, f32[4,4,32,512]{3,2,1,0:T(8,128)S(1)} %collective-permute-done.6, f32[4,4,32,512]{3,2,1,0:T(8,128)S(1)} %get-tuple-element.11), kind=kLoop, calls=%fused_computation.2 | loop fusion | flops 131072 | bytes 1048576 | tf_op jit(solution)/shard_map/add | solution.py:156
  34.4 4.3 %collective-permute-start.8 = (f32[1,4,32,512]{3,2,1,0:T(8,128)S(1)}, f32[1,4,32,512]{3,2,1,0:T(8,128)S(1)}, u32[]{:S(2)}, u32[]{:S(2)}) collective-permute-start(f32[1,4,32,512]{3,2,1,0:T(8,128)S(1)} %slice_add_fusion.2), channel_id=1, source_target_pairs={{0,16},{4,12},{8,24},{12,4},{16,0},{20,28},{24,8},{28,20},{1,17},{... | collective-permute-start | bytes 786440 | tf_op jit(solution)/shard_map/ppermute | solution.py:156
  38.7 1.6 %constant_dynamic-slice_fusion.psi_ref = f32[1,64,512]{2,1,0:T(8,128)} fusion(f32[1,512,512]{2,1,0:T(8,128)} %psi_ref.3, s32[]{:T(128)S(6)} %select_n.3), kind=kLoop, calls=%fused_computation.46 | loop fusion | bytes 262148 | tf_op jit(solution)/shard_map/dynamic_slice | solution.py:165
  40.3 1.1 %fusion.9 = (f32[32,512]{1,0:T(8,128)S(1)}, f32[32,512]{1,0:T(8,128)S(1)}, f32[32,512]{1,0:T(8,128)S(1)}) fusion(f32[1,4,32,512]{3,2,1,0:T(8,128)S(1)} %collective-permute-done.2, f32[2,4,32,512]{3,2,1,0:T(8,128)} %collective-permute-done.1, f32[4,4,32,512]{3,2,1,0:T(8,128)} %copy-done.1, f32[4,4,32,512]{3,2,1,0:T(8,128)S(1)} %get-tuple-element.9), kind=kLoop, calls=%fused_computation.35 | loop fusion | flops 147456 | bytes 983040 | tf_op jit(solution)/shard_map/add | solution.py:161
  41.4 3.3 %collective-permute-start.4 = (f32[32,512]{1,0:T(8,128)S(1)}, f32[32,512]{1,0:T(8,128)S(1)}, u32[]{:S(2)}, u32[]{:S(2)}) collective-permute-start(f32[32,512]{1,0:T(8,128)S(1)} %get-tuple-element.17), channel_id=1, source_target_pairs={{0,2},{1,3},{2,0},{3,1},{4,6},{5,7},{6,4},{7,5},{8,10},{9,11},{10,... | collective-permute-start | bytes 196616 | tf_op jit(solution)/shard_map/ppermute | solution.py:161
  44.7 1.1 %collective-permute-start.5 = (f32[32,512]{1,0:T(8,128)S(1)}, f32[32,512]{1,0:T(8,128)S(1)}, u32[]{:S(2)}, u32[]{:S(2)}) collective-permute-start(f32[32,512]{1,0:T(8,128)S(1)} %get-tuple-element.16), channel_id=1, source_target_pairs={{0,3},{1,2},{2,1},{3,0},{4,7},{5,6},{6,5},{7,4},{8,11},{9,10},{10,... | collective-permute-start | bytes 196616 | tf_op jit(solution)/shard_map/ppermute | solution.py:161
  45.8 1.0 %fusion.2 = (f32[32,512]{1,0:T(8,128)S(1)}, f32[32,512]{1,0:T(8,128)S(1)}, f32[32,512]{1,0:T(8,128)S(1)}) fusion(f32[1,4,32,512]{3,2,1,0:T(8,128)S(1)} %collective-permute-done.8, f32[2,4,32,512]{3,2,1,0:T(8,128)} %collective-permute-done.7, f32[4,4,32,512]{3,2,1,0:T(8,128)S(1)} %collective-permute-done.6, f32[4,4,32,512]{3,2,1,0:T(8,128)S(1)} %get-tuple-element.11), kind=kLoop, calls=%fused_computation.16 | loop fusion | flops 147456 | bytes 983040 | tf_op jit(solution)/shard_map/add | solution.py:161
  46.8 0.9 %collective-permute-start.10 = (f32[32,512]{1,0:T(8,128)S(1)}, f32[32,512]{1,0:T(8,128)S(1)}, u32[]{:S(2)}, u32[]{:S(2)}) collective-permute-start(f32[32,512]{1,0:T(8,128)S(1)} %get-tuple-element.20), channel_id=1, source_target_pairs={{0,2},{1,3},{2,0},{3,1},{4,6},{5,7},{6,4},{7,5},{8,10},{9,11},{10,... | collective-permute-start | bytes 196616 | tf_op jit(solution)/shard_map/ppermute | solution.py:161
  47.7 2.0 %collective-permute-start.11 = (f32[32,512]{1,0:T(8,128)S(1)}, f32[32,512]{1,0:T(8,128)S(1)}, u32[]{:S(2)}, u32[]{:S(2)}) collective-permute-start(f32[32,512]{1,0:T(8,128)S(1)} %get-tuple-element.19), channel_id=1, source_target_pairs={{0,3},{1,2},{2,1},{3,0},{4,7},{5,6},{6,5},{7,4},{8,11},{9,10},{10,... | collective-permute-start | bytes 196616 | tf_op jit(solution)/shard_map/ppermute | solution.py:161
  49.6 0.7 collective-permute-start.9
  50.9 0.9 %fusion.13 = f32[32,512]{1,0:T(8,128)S(1)} fusion(f32[32,512]{1,0:T(8,128)S(1)} %collective-permute-done.5, f32[32,512]{1,0:T(8,128)S(1)} %collective-permute-done.4, f32[32,512]{1,0:T(8,128)S(1)} %collective-permute-done.3, f32[1,4,32,512]{3,2,1,0:T(8,128)S(1)} %collective-permute-done.2, f32[2,4,32,512]{3,2,1,0:T(8,128)} %collective-permute-done.1, ...), kind=kLoop, calls=%fused_computation.42 | loop fusion | flops 98304 | bytes 524288 | tf_op jit(solution)/shard_map/add | solution.py:161
  51.8 2.4 %collective-permute-done.10 = f32[32,512]{1,0:T(8,128)S(1)} collective-permute-done((f32[32,512]{1,0:T(8,128)S(1)}, f32[32,512]{1,0:T(8,128)S(1)}, u32[]{:S(2)}, u32[]{:S(2)}) %collective-permute-start.10) | collective-permute-done | bytes 65568 | tf_op jit(solution)/shard_map/ppermute | solution.py:161
  54.8 0.9 %fusion.6 = f32[32,512]{1,0:T(8,128)S(1)} fusion(f32[32,512]{1,0:T(8,128)S(1)} %collective-permute-done.11, f32[32,512]{1,0:T(8,128)S(1)} %collective-permute-done.10, f32[32,512]{1,0:T(8,128)S(1)} %collective-permute-done.9, f32[1,4,32,512]{3,2,1,0:T(8,128)S(1)} %collective-permute-done.8, f32[2,4,32,512]{3,2,1,0:T(8,128)} %collective-permute-done.7, ...), kind=kLoop, calls=%fused_computation.23 | loop fusion | flops 98304 | bytes 524288 | tf_op jit(solution)/shard_map/add | solution.py:161
  55.7 0.7 maximum_bitcast_fusion.sigma_ref
  56.3 1.9 %stats.1 = f32[32,128]{1,0:T(8,128)} custom-call(f32[1,64,512]{2,1,0:T(8,128)} %constant_dynamic-slice_fusion.psi_ref, f32[1,64,512]{2,1,0:T(8,128)} %maximum_bitcast_fusion.sigma_ref), custom_call_target="tpu_custom_call" | custom-call | tf_op jit(solution)/shard_map/stats/pallas_call | solution.py:167
  58.3 10.2 %all_to_all.11 = f32[32,1,128]{2,1,0:T(1,128)} all-to-all(f32[32,1,128]{2,1,0:T(1,128)} %bitcast.39), channel_id=1, replica_groups=mesh['ops'=8,'sec'=4] {'ops','sec'}, dimensions={0} | all-to-all | bytes 32768 | tf_op jit(solution)/shard_map/all_to_all | solution.py:172
  68.4 2.2 %finish.1 = (f32[1,64,512]{2,1,0:T(8,128)}, f32[1,128]{1,0:T(1,128)}) custom-call(f32[1,64,512]{2,1,0:T(8,128)} %constant_dynamic-slice_fusion.psi_ref, f32[1,64,512]{2,1,0:T(8,128)} %maximum_bitcast_fusion.sigma_ref, f32[32,128]{1,0:T(8,128)} %bitcast.38), custom_call_target="tpu_custom_call" | custom-call | tf_op jit(solution)/shard_map/finish/pallas_call | solution.py:173
  70.7 1.2 %slice_bitcast_fusion = f32[2]{0:T(128)} fusion(f32[1,128]{1,0:T(1,128)} %get-tuple-element.14), kind=kLoop, calls=%fused_computation.45 | loop fusion | bytes 16 | tf_op jit(solution)/shard_map/squeeze | solution.py:181
  (13 shorter events, 1.4 us)
Async XLA Ops:
  1.4 1.2 %copy-start = (f32[1,512,512]{2,1,0:T(8,128)S(1)}, f32[1,512,512]{2,1,0:T(8,128)}, u32[]{:S(2)}) copy-start(f32[1,512,512]{2,1,0:T(8,128)} %psi_ref.3) | copy-start | bytes 3145732
  8.1 8.0 %collective-permute-start = (f32[4,4,32,512]{3,2,1,0:T(8,128)S(1)}, f32[4,4,32,512]{3,2,1,0:T(8,128)S(1)}, u32[]{:S(2)}, u32[]{:S(2)}) collective-permute-start(f32[4,4,32,512]{3,2,1,0:T(8,128)S(1)} %get-tuple-element.10), channel_id=1, source_target_pairs={{0,4},{4,0},{8,12},{12,8},{16,20},{20,16},{24,28},{28,24},{1,5},{5... | collective-permute-start | bytes 3145736 | tf_op jit(solution)/shard_map/ppermute | solution.py:152
  15.0 3.3 %collective-permute-start.6 = (f32[4,4,32,512]{3,2,1,0:T(8,128)S(1)}, f32[4,4,32,512]{3,2,1,0:T(8,128)S(1)}, u32[]{:S(2)}, u32[]{:S(2)}) collective-permute-start(f32[4,4,32,512]{3,2,1,0:T(8,128)S(1)} %get-tuple-element.12), channel_id=1, source_target_pairs={{0,4},{4,0},{8,12},{12,8},{16,20},{20,16},{24,28},{28,24},{1,5},{5... | collective-permute-start | bytes 3145736 | tf_op jit(solution)/shard_map/ppermute | solution.py:152
  16.0 2.3 %copy-start.1 = (f32[4,4,32,512]{3,2,1,0:T(8,128)}, f32[4,4,32,512]{3,2,1,0:T(8,128)S(1)}, u32[]{:S(2)}) copy-start(f32[4,4,32,512]{3,2,1,0:T(8,128)S(1)} %collective-permute-done) | copy-start | bytes 3145732
  17.0 9.5 %collective-permute-start.1 = (f32[2,4,32,512]{3,2,1,0:T(8,128)}, f32[2,4,32,512]{3,2,1,0:T(8,128)}, u32[]{:S(2)}, u32[]{:S(2)}) collective-permute-start(f32[2,4,32,512]{3,2,1,0:T(8,128)} %slice_add_fusion.1), channel_id=1, source_target_pairs={{0,8},{4,20},{8,0},{12,28},{16,24},{20,4},{24,16},{28,12},{1,9},{5... | collective-permute-start | bytes 1572872 | tf_op jit(solution)/shard_map/ppermute | solution.py:156
  19.2 14.2 %collective-permute-start.7 = (f32[2,4,32,512]{3,2,1,0:T(8,128)}, f32[2,4,32,512]{3,2,1,0:T(8,128)}, u32[]{:S(2)}, u32[]{:S(2)}) collective-permute-start(f32[2,4,32,512]{3,2,1,0:T(8,128)} %slice_add_fusion), channel_id=1, source_target_pairs={{0,8},{4,20},{8,0},{12,28},{16,24},{20,4},{24,16},{28,12},{1,9},{5... | collective-permute-start | bytes 1572872 | tf_op jit(solution)/shard_map/ppermute | solution.py:156
  27.6 12.7 %collective-permute-start.2 = (f32[1,4,32,512]{3,2,1,0:T(8,128)S(1)}, f32[1,4,32,512]{3,2,1,0:T(8,128)S(1)}, u32[]{:S(2)}, u32[]{:S(2)}) collective-permute-start(f32[1,4,32,512]{3,2,1,0:T(8,128)S(1)} %slice_add_fusion.4), channel_id=1, source_target_pairs={{0,16},{4,12},{8,24},{12,4},{16,0},{20,28},{24,8},{28,20},{1,17},{... | collective-permute-start | bytes 786440 | tf_op jit(solution)/shard_map/ppermute | solution.py:156
  34.4 11.4 %collective-permute-start.8 = (f32[1,4,32,512]{3,2,1,0:T(8,128)S(1)}, f32[1,4,32,512]{3,2,1,0:T(8,128)S(1)}, u32[]{:S(2)}, u32[]{:S(2)}) collective-permute-start(f32[1,4,32,512]{3,2,1,0:T(8,128)S(1)} %slice_add_fusion.2), channel_id=1, source_target_pairs={{0,16},{4,12},{8,24},{12,4},{16,0},{20,28},{24,8},{28,20},{1,17},{... | collective-permute-start | bytes 786440 | tf_op jit(solution)/shard_map/ppermute | solution.py:156
  41.3 8.3 %collective-permute-start.3 = (f32[32,512]{1,0:T(8,128)S(1)}, f32[32,512]{1,0:T(8,128)S(1)}, u32[]{:S(2)}, u32[]{:S(2)}) collective-permute-start(f32[32,512]{1,0:T(8,128)S(1)} %get-tuple-element.15), channel_id=1, source_target_pairs={{0,1},{1,0},{2,3},{3,2},{4,5},{5,4},{6,7},{7,6},{8,9},{9,8},{10,11... | collective-permute-start | bytes 196616 | tf_op jit(solution)/shard_map/ppermute | solution.py:161
  41.4 8.9 %collective-permute-start.4 = (f32[32,512]{1,0:T(8,128)S(1)}, f32[32,512]{1,0:T(8,128)S(1)}, u32[]{:S(2)}, u32[]{:S(2)}) collective-permute-start(f32[32,512]{1,0:T(8,128)S(1)} %get-tuple-element.17), channel_id=1, source_target_pairs={{0,2},{1,3},{2,0},{3,1},{4,6},{5,7},{6,4},{7,5},{8,10},{9,11},{10,... | collective-permute-start | bytes 196616 | tf_op jit(solution)/shard_map/ppermute | solution.py:161
  44.7 6.2 %collective-permute-start.5 = (f32[32,512]{1,0:T(8,128)S(1)}, f32[32,512]{1,0:T(8,128)S(1)}, u32[]{:S(2)}, u32[]{:S(2)}) collective-permute-start(f32[32,512]{1,0:T(8,128)S(1)} %get-tuple-element.16), channel_id=1, source_target_pairs={{0,3},{1,2},{2,1},{3,0},{4,7},{5,6},{6,5},{7,4},{8,11},{9,10},{10,... | collective-permute-start | bytes 196616 | tf_op jit(solution)/shard_map/ppermute | solution.py:161
  46.8 7.4 %collective-permute-start.10 = (f32[32,512]{1,0:T(8,128)S(1)}, f32[32,512]{1,0:T(8,128)S(1)}, u32[]{:S(2)}, u32[]{:S(2)}) collective-permute-start(f32[32,512]{1,0:T(8,128)S(1)} %get-tuple-element.20), channel_id=1, source_target_pairs={{0,2},{1,3},{2,0},{3,1},{4,6},{5,7},{6,4},{7,5},{8,10},{9,11},{10,... | collective-permute-start | bytes 196616 | tf_op jit(solution)/shard_map/ppermute | solution.py:161
  47.7 6.5 %collective-permute-start.11 = (f32[32,512]{1,0:T(8,128)S(1)}, f32[32,512]{1,0:T(8,128)S(1)}, u32[]{:S(2)}, u32[]{:S(2)}) collective-permute-start(f32[32,512]{1,0:T(8,128)S(1)} %get-tuple-element.19), channel_id=1, source_target_pairs={{0,3},{1,2},{2,1},{3,0},{4,7},{5,6},{6,5},{7,4},{8,11},{9,10},{10,... | collective-permute-start | bytes 196616 | tf_op jit(solution)/shard_map/ppermute | solution.py:161
  49.6 5.2 %collective-permute-start.9 = (f32[32,512]{1,0:T(8,128)S(1)}, f32[32,512]{1,0:T(8,128)S(1)}, u32[]{:S(2)}, u32[]{:S(2)}) collective-permute-start(f32[32,512]{1,0:T(8,128)S(1)} %get-tuple-element.18), channel_id=1, source_target_pairs={{0,1},{1,0},{2,3},{3,2},{4,5},{5,4},{6,7},{7,6},{8,9},{9,8},{10,11... | collective-permute-start | bytes 196616 | tf_op jit(solution)/shard_map/ppermute | solution.py:161

commit v2 on v1

v2 whole, which is shorter than its diff:
```python
import functools

import jax
import jax.numpy as jnp
from jax import lax
from jax.experimental import pallas as pl
from jax.experimental.pallas import tpu as pltpu
from jax.sharding import PartitionSpec as P

PIECES = (32, 32)

VMEM_BYTES = 32 * 2**20
FIFO = False
DIRECT = (True,)

NT = (((1,), (1,)), ((), ()))
NN = (((1,), (0,)), ((), ()))


def log2(n):
    bits = n.bit_length() - 1
    assert n == 1 << bits
    return bits


def bit_orders(bits):
    first = list(range(1, bits))
    turn = (bits - 1) // 2
    return first, first[turn:] + first[:turn]


def split(x):
    high = x.astype(jnp.bfloat16)
    low = (x - high.astype(jnp.float32)).astype(jnp.bfloat16)
    return high, low


def dot3(a, b_high, b_low, dims):
    a_high, a_low = split(a)
    rows = a.shape[0]
    both = lax.dot_general(
        jnp.concatenate([a_high, a_low], 0), b_high, dims, preferred_element_type=jnp.float32
    )
    cross = lax.dot_general(a_high, b_low, dims, preferred_element_type=jnp.float32)
    return both[:rows] + (both[rows:] + cross)


def sigma_kernel(
    orders, ops_bits, sectors, pieces, links_ref, psi_ref, lefts_ref, rights_ref, *rest
):
    outs = rest[: 2 * len(pieces)]
    psi, lefts, rights, psi_high, psi_low, targets, sems = rest[2 * len(pieces) :]
    pairs, _, rows, states = lefts.shape
    slots = 1 << (ops_bits - 1)
    me = lax.axis_index("ops")
    core = me & 1
    psi_copy = pltpu.make_async_copy(psi_ref.at[0], psi, sems.at[2 * pairs])
    links_copy = pltpu.make_async_copy(links_ref, targets, sems.at[2 * pairs + 1])
    left_copies = [pltpu.make_async_copy(lefts_ref.at[p], lefts.at[p], sems.at[p]) for p in range(pairs)]
    right_copies = [pltpu.make_async_copy(rights_ref.at[p], rights.at[p], sems.at[pairs + p]) for p in range(pairs)]
    links_copy.start()
    psi_copy.start()
    for p in range(pairs):
        left_copies[p].start()
        right_copies[p].start()
    for out in outs:
        out[...] = jnp.zeros_like(out)
    links_copy.wait()
    psi_copy.wait()
    high, low = split(psi[...])
    psi_high[...] = high
    psi_low[...] = low

    def contribute(pair, slot):
        blocks = []
        for away in range(2):
            owner_core = core ^ away
            for q in range(slots):
                masks = [
                    sum(1 << order[step] for step in range(ops_bits - 1) if (q >> (ops_bits - 2 - step)) & 1)
                    for order in orders
                ]
                block = me ^ away ^ jnp.where(owner_core == 0, masks[0], masks[1])
                blocks.append(lefts[pair, block])
        product_left = dot3(jnp.concatenate(blocks, 0), psi_high[...], psi_low[...], NN)
        right_high, right_low = split(rights[pair])
        product = dot3(product_left, right_high, right_low, NT)
        product = product.reshape(2, slots, rows, states)
        start = 0
        for piece, keep_ref, send_ref in zip(pieces, outs[::2], outs[1::2]):
            for q in range(slots):
                keep_ref[q, slot] += product[0, q, start : start + piece]
                send_ref[q, slot] += product[1, q, start : start + piece]
            start += piece

    for p in range(pairs):
        left_copies[p].wait()
        right_copies[p].wait()
        target = targets[p]

        @pl.when(target < sectors)
        def _():
            contribute(p, target ^ lax.axis_index("sec"))


def partial_sigma(psi, lefts, rights, links, pieces, ops_bits, sectors):
    pairs, owners, rows, states = lefts.shape
    outs = [jax.ShapeDtypeStruct((owners // 2, sectors, piece, states), jnp.float32) for piece in pieces for _ in range(2)]
    return pl.pallas_call(
        functools.partial(sigma_kernel, bit_orders(ops_bits), ops_bits, sectors, pieces),
        in_specs=[pl.BlockSpec(memory_space=pltpu.HBM)] * 4,
        out_specs=[pl.BlockSpec(memory_space=pltpu.VMEM)] * len(outs),
        out_shape=outs,
        scratch_shapes=[
            pltpu.VMEM((states, states), jnp.float32),
            pltpu.VMEM((pairs, owners, rows, states), jnp.float32),
            pltpu.VMEM((pairs, states, states), jnp.float32),
            pltpu.VMEM((states, states), jnp.bfloat16),
            pltpu.VMEM((states, states), jnp.bfloat16),
            pltpu.SMEM((pairs,), jnp.int32),
            pltpu.SemaphoreType.DMA((2 * pairs + 2,)),
        ],
        compiler_params=pltpu.CompilerParams(vmem_limit_bytes=VMEM_BYTES),
        cost_estimate=pl.CostEstimate(
            flops=12 * pairs * owners * rows * states * states,
            bytes_accessed=4 * states * states * (2 * pairs + 1),
            transcendentals=0,
        ),
        name="partial_sigma",
    )(*[pltpu.with_memory_space_constraint(x, pltpu.HBM) for x in (links, psi, lefts, rights)])


def stats_kernel(groups, psi_ref, *rest):
    ins, (sigma_ref, held_ref, psi_rows_ref, stats_ref, sem) = rest[:-5], rest[-5:]
    rows = sigma_ref.shape[1]
    copy = pltpu.make_async_copy(
        psi_ref.at[0, pl.ds(pl.multiple_of(lax.axis_index("ops") * rows, rows), rows)], psi_rows_ref, sem
    )
    copy.start()
    at = 0
    start = 0
    for group in groups:
        total = ins[at][...]
        for ref in ins[at + 1 : at + group]:
            total = total + ref[...]
        at += group
        total = total.reshape(total.shape[-2:])
        held_ref[start : start + total.shape[0]] = total
        start += total.shape[0]
    copy.wait()
    psi = psi_rows_ref[...]
    sigma = held_ref[...]
    sigma_ref[0] = sigma
    weight = jnp.sum(psi * psi)
    correlation = jnp.sum(psi * sigma)
    theta = jnp.where(weight > 0.0, correlation / weight, 0.0)
    residual = sigma - theta * psi
    squared = jnp.sum(residual * residual)
    lane = lax.broadcasted_iota(jnp.int32, stats_ref.shape, 1)
    stats_ref[...] = jnp.where(lane == 0, weight, jnp.where(lane == 1, theta, jnp.where(lane == 2, squared, 0.0)))


def finish_kernel(psi_ref, sigma_ref, stats_ref, direction_ref, energies_ref):
    weights = stats_ref[:, 0:1]
    thetas = stats_ref[:, 1:2]
    squares = stats_ref[:, 2:3]
    theta = jnp.sum(weights * thetas) / jnp.sum(weights)
    apart = thetas - theta
    norm = jnp.sqrt(jnp.sum(squares + weights * apart * apart))
    energies_ref[0] = theta
    energies_ref[1] = norm
    direction_ref[0] = (sigma_ref[...] - theta * psi_ref[...]) / norm


def after(value, earlier):
    if earlier is None:
        return value
    return lax.optimization_barrier((value, earlier))[0]


def local(psi, left_ops, right_ops, links):
    ops_width = lax.axis_size("ops")
    sectors = lax.axis_size("sec")
    ops_bits = log2(ops_width)
    sec_bits = log2(sectors)
    pairs, _, states, _ = left_ops.shape
    rows = states // ops_width
    lefts = left_ops.reshape(pairs, ops_width, rows, states)
    rights = right_ops.reshape(pairs, states, states)
    links = links.reshape(pairs)
    orders = bit_orders(ops_bits)
    pieces = PIECES if sum(PIECES) == rows else (rows // 2, rows // 2)
    partials = partial_sigma(psi, lefts, rights, links, pieces, ops_bits, sectors)
    terms = []
    groups = []
    came = None
    for index, keep, send in zip(range(len(pieces)), partials[::2], partials[1::2]):
        parts = [keep, lax.ppermute(send, "ops", [(i, i ^ 1) for i in range(ops_width)])]
        for step in range(ops_bits - 1):
            half = parts[0].shape[0] // 2
            partner = [(i, i ^ (1 << orders[i & 1][step])) for i in range(ops_width)]
            leaving = sum(p[half:] for p in parts)
            if step == 0 and FIFO:
                leaving = after(leaving, came)
            arrived = lax.ppermute(leaving, "ops", partner)
            if step == 0:
                came = arrived
            parts = [p[:half] for p in parts] + [arrived]
        parts = [p[0] for p in parts]
        if DIRECT[index % len(DIRECT)]:
            parts += [
                lax.ppermute(sum(p[q] for p in parts), "sec", [(i, i ^ q) for i in range(sectors)])
                for q in range(1, sectors)
            ]
        else:
            for bit in range(sec_bits):
                low = sectors >> (sec_bits - bit)
                picked = [q for q in range(sectors) if q & ((1 << (bit + 1)) - 1) == 1 << bit]
                kept = [q for q in range(sectors) if q & ((1 << (bit + 1)) - 1) == 0]
                if bit == 0:
                    parts = [[p[q] for q in range(sectors)] for p in parts]
                leaving = jnp.stack([sum(p[q] for p in parts) for q in picked])
                arrived = lax.ppermute(leaving, "sec", [(i, i ^ (1 << bit)) for i in range(sectors)])
                slot = dict(zip(kept, range(len(kept))))
                parts = parts + [[arrived[slot[q]] if q in slot else None for q in range(sectors)]]
            parts = [p[0][None] for p in parts]
        terms += [p[0] for p in parts[: len(parts)]] if not DIRECT[index % len(DIRECT)] else [p[0] if p.ndim == 3 else p for p in parts]
        groups.append(len(parts))
    devices = ops_width * sectors
    vmem = pl.BlockSpec(memory_space=pltpu.VMEM)
    sigma, held, psi_rows, stats = pl.pallas_call(
        functools.partial(stats_kernel, groups),
        in_specs=[pl.BlockSpec(memory_space=pltpu.HBM)] + [vmem] * len(terms),
        out_specs=[vmem] * 4,
        out_shape=[
            jax.ShapeDtypeStruct((1, rows, states), jnp.float32),
            jax.ShapeDtypeStruct((rows, states), jnp.float32),
            jax.ShapeDtypeStruct((rows, states), jnp.float32),
            jax.ShapeDtypeStruct((devices, 128), jnp.float32),
        ],
        scratch_shapes=[pltpu.SemaphoreType.DMA],
        compiler_params=pltpu.CompilerParams(vmem_limit_bytes=8 * 2**20),
        name="stats",
    )(psi, *terms)
    stats = lax.all_to_all(stats, ("ops", "sec"), 0, 0, tiled=True)
    direction, energies = pl.pallas_call(
        finish_kernel,
        in_specs=[vmem] * 3,
        out_specs=[vmem, pl.BlockSpec(memory_space=pltpu.SMEM)],
        out_shape=[
            jax.ShapeDtypeStruct((1, rows, states), jnp.float32),
            jax.ShapeDtypeStruct((2,), jnp.float32),
        ],
        compiler_params=pltpu.CompilerParams(vmem_limit_bytes=4 * 2**20),
        name="finish",
    )(psi_rows, held, stats)
    return (sigma, direction, energies)


def solution(mesh):
    return jax.shard_map(
        local,
        mesh=mesh,
        in_specs=(
            P("sec", None, None),
            P("ops", "sec", None, None),
            P("ops", "sec", None, None),
            P("ops", "sec"),
        ),
        out_specs=(P("sec", "ops", None), P("sec", "ops", None), P()),
        check_vma=False,
    )
```

time: 72.7 us -> 60 us (0.83)
  other arithmetic: 8.43 us -> 0.48 us
  Pallas kernels: 15.1 us -> 7.16 us
  waiting for transfers between devices: 12.3 us -> 18.5 us
  local copies, waits for them, and re-layouts: 4.72 us -> 0.01 us
  starting transfers between devices: 20.5 us -> 22.2 us
    pallas_call x2 -> x1, Pallas kernels: 11 us -> 4.99 us  [partial_sigma(): pl.pallas_call(functools.partial(sigma_kernel, bit_orders(ops_bits), ops_...]
    add x6 -> x4, other arithmetic: 5.73 us -> 0.3 us  [local(): leaving = sum((p[half:] for p in parts))]
    ppermute x4, waiting for transfers between devices: 8.58 us -> 11.9 us  [local(): arrived = lax.ppermute(leaving, 'ops', partner)]
    ppermute x2, waiting for transfers between devices: 0.15 us -> 2.21 us  [local(): lax.ppermute(send, 'ops', [(i, i ^ 1) for i in range(ops_width)])]
    pallas_call x2, Pallas kernels: 4.15 us -> 2.17 us  [the longest x1 1.28 us: local(): pl.pallas_call(finish_kernel, in_specs=[vmem] * 3, out_specs=[vmem, pl.Bl...]
    unnamed x5 -> x2, local copies, waits for them, and re-layouts: 1.97 us -> 0.01 us
    add x2, other arithmetic: 2.04 us -> 0.18 us  [local(): sum((p[q] for p in parts))]
    dynamic_slice x1 -> x0, local copies, waits for them, and re-layouts: 1.57 us -> none  [local(): psi_rows = lax.dynamic_slice_in_dim(psi, index * rows, rows, 1)]
  transfers between devices with their start and end apart: 12 -> 12, of which waited for: 6 -> 7; matrix products, arithmetic and copies ran while one was open for 12% -> 1% of each run, Pallas kernels for 8% -> 0%
where the time goes in v2:
time: 60 us; the launch traced here: 59.6 us
  starting transfers between devices  22.2 us (37%)
  waiting for transfers between devices  18.5 us (31%)
  blocking collectives  10.6 us (18%)
  Pallas kernels  7.16 us (12%)
  between operations  0.69 us (1%)
    ppermute x4, waiting for transfers between devices, local(): arrived = lax.ppermute(leaving, 'ops', partner)  11.9 us
    ppermute x4, starting transfers between devices, local(): arrived = lax.ppermute(leaving, 'ops', partner)  11.5 us
    all_to_all x1, blocking collectives, local(): stats = lax.all_to_all(stats, ('ops', 'sec'), 0, 0, tiled=True)  10.6 us
    ppermute x6, starting transfers between devices, local(): lax.ppermute(sum((p[q] for p in parts)), 'sec', [(i, i ^ q) for i in rang...  8.91 us
    pallas_call x1, Pallas kernels, partial_sigma(): pl.pallas_call(functools.partial(sigma_kernel, bit_orders(ops_bits), ops_...  4.99 us
    ppermute x6, waiting for transfers between devices, local(): lax.ppermute(sum((p[q] for p in parts)), 'sec', [(i, i ^ q) for i in rang...  4.37 us
    ppermute x2, waiting for transfers between devices, local(): lax.ppermute(send, 'ops', [(i, i ^ 1) for i in range(ops_width)])  2.21 us
    ppermute x2, starting transfers between devices, local(): lax.ppermute(send, 'ops', [(i, i ^ 1) for i in range(ops_width)])  1.77 us
  transfers between devices with their start and end apart: 12, of which 7 were waited for; matrix products, arithmetic and copies ran while one was open for 1% of the time, Pallas kernels for 0%

profile of v2, /device:TPU:0, one launch (start us, length us, event | category | flops | bytes accessed | tf_op | source)
XLA Modules:
  0.0 59.6 jit_solution(12271337724603365987)
XLA Ops:
  0.6 5.0 %partial_sigma.1 = (f32[4,4,32,512]{3,2,1,0:T(8,128)S(1)}, f32[4,4,32,512]{3,2,1,0:T(8,128)S(1)}, f32[4,4,32,512]{3,2,1,0:T(8,128)S(1)}, f32[4,4,32,512]{3,2,1,0:T(8,128)S(1)}) custom-call(s32[4]{0:T(128)} %bitcast.39, f32[1,512,512]{2,1,0:T(8,128)} %psi_ref.3, f32[4,8,64,512]{3,2,1,0:T(8,128)} %bitcast.37, f32[4,512,512]{2,1,0:T(8,128)} %bitcast.38), custom_call_target="tpu_custom_call" | custom-call | flops 6442450944 | bytes 9437184 | tf_op jit(solution)/shard_map/partial_sigma/pallas_call | solution.py:109
  5.6 0.0 copy-start
  5.6 1.7 %collective-permute-start = (f32[4,4,32,512]{3,2,1,0:T(8,128)S(1)}, f32[4,4,32,512]{3,2,1,0:T(8,128)S(1)}, u32[]{:S(2)}, u32[]{:S(2)}) collective-permute-start(f32[4,4,32,512]{3,2,1,0:T(8,128)S(1)} %get-tuple-element.14), channel_id=1, source_target_pairs={{0,4},{4,0},{8,12},{12,8},{16,20},{20,16},{24,28},{28,24},{1,5},{5... | collective-permute-start | bytes 3145736 | tf_op jit(solution)/shard_map/ppermute | solution.py:198
  7.3 0.1 collective-permute-start.6
  7.4 2.2 %collective-permute-done = f32[4,4,32,512]{3,2,1,0:T(8,128)S(1)} collective-permute-done((f32[4,4,32,512]{3,2,1,0:T(8,128)S(1)}, f32[4,4,32,512]{3,2,1,0:T(8,128)S(1)}, u32[]{:S(2)}, u32[]{:S(2)}) %collective-permute-start) | collective-permute-done | bytes 1048608 | tf_op jit(solution)/shard_map/ppermute | solution.py:198
  9.6 0.1 slice_add_fusion.1
  9.7 5.9 %collective-permute-start.1 = (f32[2,4,32,512]{3,2,1,0:T(8,128)S(1)}, f32[2,4,32,512]{3,2,1,0:T(8,128)S(1)}, u32[]{:S(2)}, u32[]{:S(2)}) collective-permute-start(f32[2,4,32,512]{3,2,1,0:T(8,128)S(1)} %slice_add_fusion.1), channel_id=1, source_target_pairs={{0,8},{4,20},{8,0},{12,28},{16,24},{20,4},{24,16},{28,12},{1,9},{5... | collective-permute-start | bytes 1572872 | tf_op jit(solution)/shard_map/ppermute | solution.py:205
  15.6 0.0 collective-permute-done.6
  15.6 0.1 slice_add_fusion
  15.7 1.4 %collective-permute-start.7 = (f32[2,4,32,512]{3,2,1,0:T(8,128)S(1)}, f32[2,4,32,512]{3,2,1,0:T(8,128)S(1)}, u32[]{:S(2)}, u32[]{:S(2)}) collective-permute-start(f32[2,4,32,512]{3,2,1,0:T(8,128)S(1)} %slice_add_fusion), channel_id=1, source_target_pairs={{0,8},{4,20},{8,0},{12,28},{16,24},{20,4},{24,16},{28,12},{1,9},{5... | collective-permute-start | bytes 1572872 | tf_op jit(solution)/shard_map/ppermute | solution.py:205
  17.1 5.7 %collective-permute-done.1 = f32[2,4,32,512]{3,2,1,0:T(8,128)S(1)} collective-permute-done((f32[2,4,32,512]{3,2,1,0:T(8,128)S(1)}, f32[2,4,32,512]{3,2,1,0:T(8,128)S(1)}, u32[]{:S(2)}, u32[]{:S(2)}) %collective-permute-start.1) | collective-permute-done | bytes 524320 | tf_op jit(solution)/shard_map/ppermute | solution.py:205
  22.7 0.1 slice_add_fusion.4
  22.8 2.1 %collective-permute-start.2 = (f32[1,4,32,512]{3,2,1,0:T(8,128)S(1)}, f32[1,4,32,512]{3,2,1,0:T(8,128)S(1)}, u32[]{:S(2)}, u32[]{:S(2)}) collective-permute-start(f32[1,4,32,512]{3,2,1,0:T(8,128)S(1)} %slice_add_fusion.4), channel_id=1, source_target_pairs={{0,16},{4,12},{8,24},{12,4},{16,0},{20,28},{24,8},{28,20},{1,17},{... | collective-permute-start | bytes 786440 | tf_op jit(solution)/shard_map/ppermute | solution.py:205
  24.9 6.2 %collective-permute-done.7 = f32[2,4,32,512]{3,2,1,0:T(8,128)S(1)} collective-permute-done((f32[2,4,32,512]{3,2,1,0:T(8,128)S(1)}, f32[2,4,32,512]{3,2,1,0:T(8,128)S(1)}, u32[]{:S(2)}, u32[]{:S(2)}) %collective-permute-start.7) | collective-permute-done | bytes 524320 | tf_op jit(solution)/shard_map/ppermute | solution.py:205
  31.2 0.1 slice_add_fusion.2
  31.2 2.1 %collective-permute-start.8 = (f32[1,4,32,512]{3,2,1,0:T(8,128)S(1)}, f32[1,4,32,512]{3,2,1,0:T(8,128)S(1)}, u32[]{:S(2)}, u32[]{:S(2)}) collective-permute-start(f32[1,4,32,512]{3,2,1,0:T(8,128)S(1)} %slice_add_fusion.2), channel_id=1, source_target_pairs={{0,16},{4,12},{8,24},{12,4},{16,0},{20,28},{24,8},{28,20},{1,17},{... | collective-permute-start | bytes 786440 | tf_op jit(solution)/shard_map/ppermute | solution.py:205
  33.3 0.0 collective-permute-done.2
  33.3 0.1 fusion.3
  33.4 3.7 %collective-permute-start.5 = (f32[32,512]{1,0:T(8,128)S(1)}, f32[32,512]{1,0:T(8,128)S(1)}, u32[]{:S(2)}, u32[]{:S(2)}) collective-permute-start(f32[32,512]{1,0:T(8,128)S(1)} %get-tuple-element.26), channel_id=1, source_target_pairs={{0,3},{1,2},{2,1},{3,0},{4,7},{5,6},{6,5},{7,4},{8,11},{9,10},{10,... | collective-permute-start | bytes 196616 | tf_op jit(solution)/shard_map/ppermute | solution.py:212
  37.1 0.8 %collective-permute-start.3 = (f32[32,512]{1,0:T(8,128)S(1)}, f32[32,512]{1,0:T(8,128)S(1)}, u32[]{:S(2)}, u32[]{:S(2)}) collective-permute-start(f32[32,512]{1,0:T(8,128)S(1)} %get-tuple-element.28), channel_id=1, source_target_pairs={{0,1},{1,0},{2,3},{3,2},{4,5},{5,4},{6,7},{7,6},{8,9},{9,8},{10,11... | collective-permute-start | bytes 196616 | tf_op jit(solution)/shard_map/ppermute | solution.py:212
  37.9 0.1 fusion
  38.0 3.7 %collective-permute-start.11 = (f32[32,512]{1,0:T(8,128)S(1)}, f32[32,512]{1,0:T(8,128)S(1)}, u32[]{:S(2)}, u32[]{:S(2)}) collective-permute-start(f32[32,512]{1,0:T(8,128)S(1)} %get-tuple-element.23), channel_id=1, source_target_pairs={{0,3},{1,2},{2,1},{3,0},{4,7},{5,6},{6,5},{7,4},{8,11},{9,10},{10,... | collective-permute-start | bytes 196616 | tf_op jit(solution)/shard_map/ppermute | solution.py:212
  41.6 0.0 collective-permute-start.10
  41.7 0.8 %collective-permute-start.9 = (f32[32,512]{1,0:T(8,128)S(1)}, f32[32,512]{1,0:T(8,128)S(1)}, u32[]{:S(2)}, u32[]{:S(2)}) collective-permute-start(f32[32,512]{1,0:T(8,128)S(1)} %get-tuple-element.25), channel_id=1, source_target_pairs={{0,1},{1,0},{2,3},{3,2},{4,5},{5,4},{6,7},{7,6},{8,9},{9,8},{10,11... | collective-permute-start | bytes 196616 | tf_op jit(solution)/shard_map/ppermute | solution.py:212
  42.4 1.4 %collective-permute-done.4.rest_5_ = f32[32,512]{1,0:T(8,128)S(1)} collective-permute-done((f32[32,512]{1,0:T(8,128)S(1)}, f32[32,512]{1,0:T(8,128)S(1)}, u32[]{:S(2)}, u32[]{:S(2)}) %collective-permute-start.4) | collective-permute-done | bytes 65568 | tf_op jit(solution)/shard_map/ppermute | solution.py:212
  43.9 0.2 collective-permute-done.3.rest_4_
  44.0 0.9 %collective-permute-done.11.rest_13_ = f32[32,512]{1,0:T(8,128)S(1)} collective-permute-done((f32[32,512]{1,0:T(8,128)S(1)}, f32[32,512]{1,0:T(8,128)S(1)}, u32[]{:S(2)}, u32[]{:S(2)}) %collective-permute-start.11) | collective-permute-done | bytes 65568 | tf_op jit(solution)/shard_map/ppermute | solution.py:212
  44.9 1.9 %collective-permute-done.10.rest_12_ = f32[32,512]{1,0:T(8,128)S(1)} collective-permute-done((f32[32,512]{1,0:T(8,128)S(1)}, f32[32,512]{1,0:T(8,128)S(1)}, u32[]{:S(2)}, u32[]{:S(2)}) %collective-permute-start.10) | collective-permute-done | bytes 65568 | tf_op jit(solution)/shard_map/ppermute | solution.py:212
  46.8 0.0 collective-permute-done.9.rest_11_
  46.8 0.9 %stats.1 = (f32[1,64,512]{2,1,0:T(8,128)}, f32[64,512]{1,0:T(8,128)S(1)}, f32[64,512]{1,0:T(8,128)S(1)}, f32[32,128]{1,0:T(8,128)S(1)}) custom-call(f32[1,512,512]{2,1,0:T(8,128)S(1)} %copy-done, f32[32,512]{1,0:T(8,128)S(1)} %get-tuple-element.31.rest_0_, f32[32,512]{1,0:T(8,128)S(1)} %get-tuple-element.32.rest_1_, ...), custom_call_target="tpu_custom_call" | custom-call | tf_op jit(solution)/shard_map/stats/pallas_call | solution.py:231
  47.7 10.6 %all_to_all.11 = f32[32,1,128]{2,1,0:T(1,128)S(1)} all-to-all(f32[32,1,128]{2,1,0:T(1,128)S(1)} %bitcast.36), channel_id=1, replica_groups=mesh['ops'=8,'sec'=4] {'ops','sec'}, dimensions={0} | all-to-all | bytes 32768 | tf_op jit(solution)/shard_map/all_to_all | solution.py:245
  58.3 1.3 %finish.1 = (f32[1,64,512]{2,1,0:T(8,128)}, f32[2]{0:T(128)}) custom-call(f32[64,512]{1,0:T(8,128)S(1)} %get-tuple-element.18.psi_ref, f32[64,512]{1,0:T(8,128)S(1)} %get-tuple-element.19.sigma_ref, f32[32,128]{1,0:T(8,128)S(1)} %bitcast.35), custom_call_target="tpu_custom_call" | custom-call | tf_op jit(solution)/shard_map/finish/pallas_call | solution.py:246
  (4 shorter events, 0.0 us)
Async XLA Ops:
  5.6 41.2 %copy-start = (f32[1,512,512]{2,1,0:T(8,128)S(1)}, f32[1,512,512]{2,1,0:T(8,128)}, u32[]{:S(2)}) copy-start(f32[1,512,512]{2,1,0:T(8,128)} %psi_ref.3) | copy-start | bytes 3145732
  5.6 4.0 %collective-permute-start = (f32[4,4,32,512]{3,2,1,0:T(8,128)S(1)}, f32[4,4,32,512]{3,2,1,0:T(8,128)S(1)}, u32[]{:S(2)}, u32[]{:S(2)}) collective-permute-start(f32[4,4,32,512]{3,2,1,0:T(8,128)S(1)} %get-tuple-element.14), channel_id=1, source_target_pairs={{0,4},{4,0},{8,12},{12,8},{16,20},{20,16},{24,28},{28,24},{1,5},{5... | collective-permute-start | bytes 3145736 | tf_op jit(solution)/shard_map/ppermute | solution.py:198
  7.3 8.2 %collective-permute-start.6 = (f32[4,4,32,512]{3,2,1,0:T(8,128)S(1)}, f32[4,4,32,512]{3,2,1,0:T(8,128)S(1)}, u32[]{:S(2)}, u32[]{:S(2)}) collective-permute-start(f32[4,4,32,512]{3,2,1,0:T(8,128)S(1)} %get-tuple-element.16), channel_id=1, source_target_pairs={{0,4},{4,0},{8,12},{12,8},{16,20},{20,16},{24,28},{28,24},{1,5},{5... | collective-permute-start | bytes 3145736 | tf_op jit(solution)/shard_map/ppermute | solution.py:198
  9.7 13.0 %collective-permute-start.1 = (f32[2,4,32,512]{3,2,1,0:T(8,128)S(1)}, f32[2,4,32,512]{3,2,1,0:T(8,128)S(1)}, u32[]{:S(2)}, u32[]{:S(2)}) collective-permute-start(f32[2,4,32,512]{3,2,1,0:T(8,128)S(1)} %slice_add_fusion.1), channel_id=1, source_target_pairs={{0,8},{4,20},{8,0},{12,28},{16,24},{20,4},{24,16},{28,12},{1,9},{5... | collective-permute-start | bytes 1572872 | tf_op jit(solution)/shard_map/ppermute | solution.py:205
  15.7 15.5 %collective-permute-start.7 = (f32[2,4,32,512]{3,2,1,0:T(8,128)S(1)}, f32[2,4,32,512]{3,2,1,0:T(8,128)S(1)}, u32[]{:S(2)}, u32[]{:S(2)}) collective-permute-start(f32[2,4,32,512]{3,2,1,0:T(8,128)S(1)} %slice_add_fusion), channel_id=1, source_target_pairs={{0,8},{4,20},{8,0},{12,28},{16,24},{20,4},{24,16},{28,12},{1,9},{5... | collective-permute-start | bytes 1572872 | tf_op jit(solution)/shard_map/ppermute | solution.py:205
  22.8 10.5 %collective-permute-start.2 = (f32[1,4,32,512]{3,2,1,0:T(8,128)S(1)}, f32[1,4,32,512]{3,2,1,0:T(8,128)S(1)}, u32[]{:S(2)}, u32[]{:S(2)}) collective-permute-start(f32[1,4,32,512]{3,2,1,0:T(8,128)S(1)} %slice_add_fusion.4), channel_id=1, source_target_pairs={{0,16},{4,12},{8,24},{12,4},{16,0},{20,28},{24,8},{28,20},{1,17},{... | collective-permute-start | bytes 786440 | tf_op jit(solution)/shard_map/ppermute | solution.py:205
  31.2 6.7 %collective-permute-start.8 = (f32[1,4,32,512]{3,2,1,0:T(8,128)S(1)}, f32[1,4,32,512]{3,2,1,0:T(8,128)S(1)}, u32[]{:S(2)}, u32[]{:S(2)}) collective-permute-start(f32[1,4,32,512]{3,2,1,0:T(8,128)S(1)} %slice_add_fusion.2), channel_id=1, source_target_pairs={{0,16},{4,12},{8,24},{12,4},{16,0},{20,28},{24,8},{28,20},{1,17},{... | collective-permute-start | bytes 786440 | tf_op jit(solution)/shard_map/ppermute | solution.py:205
  33.4 8.2 %collective-permute-start.5 = (f32[32,512]{1,0:T(8,128)S(1)}, f32[32,512]{1,0:T(8,128)S(1)}, u32[]{:S(2)}, u32[]{:S(2)}) collective-permute-start(f32[32,512]{1,0:T(8,128)S(1)} %get-tuple-element.26), channel_id=1, source_target_pairs={{0,3},{1,2},{2,1},{3,0},{4,7},{5,6},{6,5},{7,4},{8,11},{9,10},{10,... | collective-permute-start | bytes 196616 | tf_op jit(solution)/shard_map/ppermute | solution.py:212
  37.1 6.8 %collective-permute-start.4 = (f32[32,512]{1,0:T(8,128)S(1)}, f32[32,512]{1,0:T(8,128)S(1)}, u32[]{:S(2)}, u32[]{:S(2)}) collective-permute-start(f32[32,512]{1,0:T(8,128)S(1)} %get-tuple-element.27), channel_id=1, source_target_pairs={{0,2},{1,3},{2,0},{3,1},{4,6},{5,7},{6,4},{7,5},{8,10},{9,11},{10,... | collective-permute-start | bytes 196616 | tf_op jit(solution)/shard_map/ppermute | solution.py:212
  37.1 6.9 %collective-permute-start.3 = (f32[32,512]{1,0:T(8,128)S(1)}, f32[32,512]{1,0:T(8,128)S(1)}, u32[]{:S(2)}, u32[]{:S(2)}) collective-permute-start(f32[32,512]{1,0:T(8,128)S(1)} %get-tuple-element.28), channel_id=1, source_target_pairs={{0,1},{1,0},{2,3},{3,2},{4,5},{5,4},{6,7},{7,6},{8,9},{9,8},{10,11... | collective-permute-start | bytes 196616 | tf_op jit(solution)/shard_map/ppermute | solution.py:212
  38.0 7.0 %collective-permute-start.11 = (f32[32,512]{1,0:T(8,128)S(1)}, f32[32,512]{1,0:T(8,128)S(1)}, u32[]{:S(2)}, u32[]{:S(2)}) collective-permute-start(f32[32,512]{1,0:T(8,128)S(1)} %get-tuple-element.23), channel_id=1, source_target_pairs={{0,3},{1,2},{2,1},{3,0},{4,7},{5,6},{6,5},{7,4},{8,11},{9,10},{10,... | collective-permute-start | bytes 196616 | tf_op jit(solution)/shard_map/ppermute | solution.py:212
  41.6 5.2 %collective-permute-start.10 = (f32[32,512]{1,0:T(8,128)S(1)}, f32[32,512]{1,0:T(8,128)S(1)}, u32[]{:S(2)}, u32[]{:S(2)}) collective-permute-start(f32[32,512]{1,0:T(8,128)S(1)} %get-tuple-element.24), channel_id=1, source_target_pairs={{0,2},{1,3},{2,0},{3,1},{4,6},{5,7},{6,4},{7,5},{8,10},{9,11},{10,... | collective-permute-start | bytes 196616 | tf_op jit(solution)/shard_map/ppermute | solution.py:212
  41.7 5.2 %collective-permute-start.9 = (f32[32,512]{1,0:T(8,128)S(1)}, f32[32,512]{1,0:T(8,128)S(1)}, u32[]{:S(2)}, u32[]{:S(2)}) collective-permute-start(f32[32,512]{1,0:T(8,128)S(1)} %get-tuple-element.25), channel_id=1, source_target_pairs={{0,1},{1,0},{2,3},{3,2},{4,5},{5,4},{6,7},{7,6},{8,9},{9,8},{10,11... | collective-permute-start | bytes 196616 | tf_op jit(solution)/shard_map/ppermute | solution.py:212

commit v3 on v2

--- a/solution.py
+++ b/solution.py
@@ -7,11 +7,9 @@
 from jax.experimental.pallas import tpu as pltpu
 from jax.sharding import PartitionSpec as P
 
-PIECES = (32, 32)
+STREAM_P = 40
 
 VMEM_BYTES = 32 * 2**20
-FIFO = False
-DIRECT = (True,)
 
 NT = (((1,), (1,)), ((), ()))
 NN = (((1,), (0,)), ((), ()))
@@ -23,10 +21,23 @@
     return bits
 
 
-def bit_orders(bits):
-    first = list(range(1, bits))
-    turn = (bits - 1) // 2
-    return first, first[turn:] + first[:turn]
+def halving_orders(ops_bits, sec_bits):
+    plane = [("ops", bit) for bit in range(1, ops_bits)]
+    turned = plane[(ops_bits - 1) // 2 :] + plane[: (ops_bits - 1) // 2]
+    sector = [("sec", bit) for bit in range(sec_bits)]
+    return (
+        (plane + sector, turned + sector),
+        (sector[::-1] + plane, sector + turned),
+    )
+
+
+def places(order, axis):
+    last = len(order) - 1
+    return {bit: 1 << (last - step) for step, (name, bit) in enumerate(order) if name == axis}
+
+
+def slot_part(order, axis, mask):
+    return sum(((mask >> bit) & 1) * weight for bit, weight in places(order, axis).items())
 
 
 def split(x):
@@ -45,13 +56,10 @@
     return both[:rows] + (both[rows:] + cross)
 
 
-def sigma_kernel(
-    orders, ops_bits, sectors, pieces, links_ref, psi_ref, lefts_ref, rights_ref, *rest
-):
-    outs = rest[: 2 * len(pieces)]
-    psi, lefts, rights, psi_high, psi_low, targets, sems = rest[2 * len(pieces) :]
+def sigma_kernel(orders, sectors, pieces, links_ref, psi_ref, lefts_ref, rights_ref, *rest):
+    outs, (psi, lefts, rights, psi_high, psi_low, targets, sems) = rest[:4], rest[4:]
     pairs, _, rows, states = lefts.shape
-    slots = 1 << (ops_bits - 1)
+    blocks = lefts.shape[1] // 2
     me = lax.axis_index("ops")
     core = me & 1
     psi_copy = pltpu.make_async_copy(psi_ref.at[0], psi, sems.at[2 * pairs])
@@ -71,26 +79,30 @@
     psi_high[...] = high
     psi_low[...] = low
 
-    def contribute(pair, slot):
-        blocks = []
-        for away in range(2):
-            owner_core = core ^ away
-            for q in range(slots):
-                masks = [
-                    sum(1 << order[step] for step in range(ops_bits - 1) if (q >> (ops_bits - 2 - step)) & 1)
-                    for order in orders
-                ]
-                block = me ^ away ^ jnp.where(owner_core == 0, masks[0], masks[1])
-                blocks.append(lefts[pair, block])
-        product_left = dot3(jnp.concatenate(blocks, 0), psi_high[...], psi_low[...], NN)
+    def contribute(pair, away_sector):
+        mine = jnp.concatenate(
+            [lefts[pair, me ^ away ^ (block << 1)] for away in range(2) for block in range(blocks)], 0
+        )
+        product_left = dot3(mine, psi_high[...], psi_low[...], NN)
         right_high, right_low = split(rights[pair])
         product = dot3(product_left, right_high, right_low, NT)
-        product = product.reshape(2, slots, rows, states)
+        product = product.reshape(2, blocks, rows, states)
         start = 0
-        for piece, keep_ref, send_ref in zip(pieces, outs[::2], outs[1::2]):
-            for q in range(slots):
-                keep_ref[q, slot] += product[0, q, start : start + piece]
-                send_ref[q, slot] += product[1, q, start : start + piece]
+        for stream, piece in enumerate(pieces):
+            for away in range(2):
+                first = (core ^ away) == 0
+                sector_part = jnp.where(
+                    first,
+                    slot_part(orders[stream][0], "sec", away_sector),
+                    slot_part(orders[stream][1], "sec", away_sector),
+                )
+                for block in range(blocks):
+                    block_part = jnp.where(
+                        first,
+                        slot_part(orders[stream][0], "ops", block << 1),
+                        slot_part(orders[stream][1], "ops", block << 1),
+                    )
+                    outs[2 * stream + away][block_part + sector_part] += product[away, block, start : start + piece]
             start += piece
 
     for p in range(pairs):
@@ -103,11 +115,13 @@
             contribute(p, target ^ lax.axis_index("sec"))
 
 
-def partial_sigma(psi, lefts, rights, links, pieces, ops_bits, sectors):
+def partial_sigma(psi, lefts, rights, links, pieces, orders, sectors):
     pairs, owners, rows, states = lefts.shape
-    outs = [jax.ShapeDtypeStruct((owners // 2, sectors, piece, states), jnp.float32) for piece in pieces for _ in range(2)]
+    outs = [
+        jax.ShapeDtypeStruct((owners // 2 * sectors, piece, states), jnp.float32) for piece in pieces for _ in range(2)
+    ]
     return pl.pallas_call(
-        functools.partial(sigma_kernel, bit_orders(ops_bits), ops_bits, sectors, pieces),
+        functools.partial(sigma_kernel, orders, sectors, pieces),
         in_specs=[pl.BlockSpec(memory_space=pltpu.HBM)] * 4,
         out_specs=[pl.BlockSpec(memory_space=pltpu.VMEM)] * len(outs),
         out_shape=outs,
@@ -172,60 +186,38 @@
     direction_ref[0] = (sigma_ref[...] - theta * psi_ref[...]) / norm
 
 
-def after(value, earlier):
-    if earlier is None:
-        return value
-    return lax.optimization_barrier((value, earlier))[0]
+def halve(parts, orders, ops_width, sectors):
+    for step in range(len(orders[0])):
+        partner = []
+        for ops in range(ops_width):
+            axis, bit = orders[ops & 1][step]
+            for sec in range(sectors):
+                to = (ops ^ (1 << bit), sec) if axis == "ops" else (ops, sec ^ (1 << bit))
+                partner.append((ops * sectors + sec, to[0] * sectors + to[1]))
+        half = parts[0].shape[0] // 2
+        leaving = sum(p[half:] for p in parts)
+        parts = [p[:half] for p in parts] + [lax.ppermute(leaving, ("ops", "sec"), partner)]
+    return [p[0] for p in parts]
 
 
 def local(psi, left_ops, right_ops, links):
     ops_width = lax.axis_size("ops")
     sectors = lax.axis_size("sec")
-    ops_bits = log2(ops_width)
-    sec_bits = log2(sectors)
     pairs, _, states, _ = left_ops.shape
     rows = states // ops_width
     lefts = left_ops.reshape(pairs, ops_width, rows, states)
     rights = right_ops.reshape(pairs, states, states)
     links = links.reshape(pairs)
-    orders = bit_orders(ops_bits)
-    pieces = PIECES if sum(PIECES) == rows else (rows // 2, rows // 2)
-    partials = partial_sigma(psi, lefts, rights, links, pieces, ops_bits, sectors)
-    terms = []
-    groups = []
-    came = None
-    for index, keep, send in zip(range(len(pieces)), partials[::2], partials[1::2]):
-        parts = [keep, lax.ppermute(send, "ops", [(i, i ^ 1) for i in range(ops_width)])]
-        for step in range(ops_bits - 1):
-            half = parts[0].shape[0] // 2
-            partner = [(i, i ^ (1 << orders[i & 1][step])) for i in range(ops_width)]
-            leaving = sum(p[half:] for p in parts)
-            if step == 0 and FIFO:
-                leaving = after(leaving, came)
-            arrived = lax.ppermute(leaving, "ops", partner)
-            if step == 0:
-                came = arrived
-            parts = [p[:half] for p in parts] + [arrived]
-        parts = [p[0] for p in parts]
-        if DIRECT[index % len(DIRECT)]:
-            parts += [
-                lax.ppermute(sum(p[q] for p in parts), "sec", [(i, i ^ q) for i in range(sectors)])
-                for q in range(1, sectors)
-            ]
-        else:
-            for bit in range(sec_bits):
-                low = sectors >> (sec_bits - bit)
-                picked = [q for q in range(sectors) if q & ((1 << (bit + 1)) - 1) == 1 << bit]
-                kept = [q for q in range(sectors) if q & ((1 << (bit + 1)) - 1) == 0]
-                if bit == 0:
-                    parts = [[p[q] for q in range(sectors)] for p in parts]
-                leaving = jnp.stack([sum(p[q] for p in parts) for q in picked])
-                arrived = lax.ppermute(leaving, "sec", [(i, i ^ (1 << bit)) for i in range(sectors)])
-                slot = dict(zip(kept, range(len(kept))))
-                parts = parts + [[arrived[slot[q]] if q in slot else None for q in range(sectors)]]
-            parts = [p[0][None] for p in parts]
-        terms += [p[0] for p in parts[: len(parts)]] if not DIRECT[index % len(DIRECT)] else [p[0] if p.ndim == 3 else p for p in parts]
-        groups.append(len(parts))
+    orders = halving_orders(log2(ops_width), log2(sectors))
+    pieces = (STREAM_P, rows - STREAM_P) if rows > STREAM_P else (rows // 2, rows - rows // 2)
+    keep_p, send_p, keep_q, send_q = partial_sigma(psi, lefts, rights, links, pieces, orders, sectors)
+    swap = [(i, i ^ 1) for i in range(ops_width)]
+    came_p = lax.ppermute(send_p, "ops", swap)
+    came_q = lax.ppermute(send_q, "ops", swap)
+    stream_p = halve([keep_p, came_p], orders[0], ops_width, sectors)
+    stream_q = halve([keep_q, came_q], orders[1], ops_width, sectors)
+    terms = stream_p + stream_q
+    groups = [len(stream_p), len(stream_q)]
     devices = ops_width * sectors
     vmem = pl.BlockSpec(memory_space=pltpu.VMEM)
     sigma, held, psi_rows, stats = pl.pallas_call(

time: 60 us -> 59.7 us (level)
  blocking collectives: 10.6 us -> 12.6 us
  starting transfers between devices: 22.2 us -> 20.4 us
  waiting for transfers between devices: 18.5 us -> 17.9 us
    all_to_all x1, blocking collectives: 10.6 us -> 12.6 us  [local(): stats = lax.all_to_all(stats, ('ops', 'sec'), 0, 0, tiled=True)]
    ppermute x12 -> x10, starting transfers between devices: 22.2 us -> 20.4 us  [the longest x8 19.9 us: halve(): lax.ppermute(leaving, ('ops', 'sec'), partner)]
    ppermute x12 -> x10, waiting for transfers between devices: 18.5 us -> 17.9 us  [the longest x8 15.4 us: halve(): lax.ppermute(leaving, ('ops', 'sec'), partner)]
  transfers between devices with their start and end apart: 12 -> 10, of which waited for: 7 -> 8; matrix products, arithmetic and copies ran while one was open for 1% -> 1% of each run, Pallas kernels for 0% -> 0%
where the time goes in v3:
time: 59.7 us; the launch traced here: 59.9 us
  starting transfers between devices  20.4 us (34%)
  waiting for transfers between devices  17.9 us (30%)
  blocking collectives  12.6 us (21%)
  Pallas kernels  7.73 us (13%)
  between operations  0.69 us (1%)
    ppermute x8, starting transfers between devices, halve(): lax.ppermute(leaving, ('ops', 'sec'), partner)  19.9 us
    ppermute x8, waiting for transfers between devices, halve(): lax.ppermute(leaving, ('ops', 'sec'), partner)  15.4 us
    all_to_all x1, blocking collectives, local(): stats = lax.all_to_all(stats, ('ops', 'sec'), 0, 0, tiled=True)  12.6 us
    pallas_call x1, Pallas kernels, partial_sigma(): pl.pallas_call(functools.partial(sigma_kernel, orders, sectors, pieces),...  5.58 us
    ppermute x1, waiting for transfers between devices, local(): came_p = lax.ppermute(send_p, 'ops', swap)  2.56 us
    pallas_call x1, Pallas kernels, local(): pl.pallas_call(finish_kernel, in_specs=[vmem] * 3, out_specs=[vmem, pl.Bl...  1.28 us
  transfers between devices with their start and end apart: 10, of which 8 were waited for; matrix products, arithmetic and copies ran while one was open for 1% of the time, Pallas kernels for 0%

profile of v3, /device:TPU:0, one launch (start us, length us, event | category | flops | bytes accessed | tf_op | source)
XLA Modules:
  0.0 59.9 jit_solution(6314866232114481823)
XLA Ops:
  0.6 5.6 %partial_sigma.1 = (f32[16,40,512]{2,1,0:T(8,128)S(1)}, f32[16,40,512]{2,1,0:T(8,128)S(1)}, f32[16,24,512]{2,1,0:T(8,128)S(1)}, f32[16,24,512]{2,1,0:T(8,128)S(1)}) custom-call(s32[4]{0:T(128)} %bitcast.35, f32[1,512,512]{2,1,0:T(8,128)} %psi_ref.3, f32[4,8,64,512]{3,2,1,0:T(8,128)} %bitcast.33, f32[4,512,512]{2,1,0:T(8,128)} %bitcast.34), custom_call_target="tpu_custom_call" | custom-call | flops 6442450944 | bytes 9437184 | tf_op jit(solution)/shard_map/partial_sigma/pallas_call | solution.py:123
  6.2 0.5 collective-permute-start
  6.7 0.1 collective-permute-start.5
  6.8 2.6 %collective-permute-done = f32[16,40,512]{2,1,0:T(8,128)S(1)} collective-permute-done((f32[16,40,512]{2,1,0:T(8,128)S(1)}, f32[16,40,512]{2,1,0:T(8,128)S(1)}, u32[]{:S(2)}, u32[]{:S(2)}) %collective-permute-start) | collective-permute-done | bytes 1310752 | tf_op jit(solution)/shard_map/ppermute | solution.py:215
  9.4 0.1 slice_add_fusion
  9.5 4.7 %collective-permute-start.1 = (f32[8,40,512]{2,1,0:T(8,128)S(1)}, f32[8,40,512]{2,1,0:T(8,128)S(1)}, u32[]{:S(2)}, u32[]{:S(2)}) collective-permute-start(f32[8,40,512]{2,1,0:T(8,128)S(1)} %slice_add_fusion), channel_id=1, source_target_pairs={{0,8},{1,9},{2,10},{3,11},{4,20},{5,21},{6,22},{7,23},{8,0},{9,1},... | collective-permute-start | bytes 1966088 | tf_op jit(solution)/shard_map/ppermute | solution.py:199
  14.2 0.0 collective-permute-done.5
  14.2 0.1 slice_add_fusion.1
  14.2 2.7 %collective-permute-start.6 = (f32[8,24,512]{2,1,0:T(8,128)S(1)}, f32[8,24,512]{2,1,0:T(8,128)S(1)}, u32[]{:S(2)}, u32[]{:S(2)}) collective-permute-start(f32[8,24,512]{2,1,0:T(8,128)S(1)} %slice_add_fusion.1), channel_id=1, source_target_pairs={{0,2},{1,3},{2,0},{3,1},{4,5},{5,4},{6,7},{7,6},{8,10},{9,11},{10,... | collective-permute-start | bytes 1179656 | tf_op jit(solution)/shard_map/ppermute | solution.py:199
  16.9 5.8 %collective-permute-done.1 = f32[8,40,512]{2,1,0:T(8,128)S(1)} collective-permute-done((f32[8,40,512]{2,1,0:T(8,128)S(1)}, f32[8,40,512]{2,1,0:T(8,128)S(1)}, u32[]{:S(2)}, u32[]{:S(2)}) %collective-permute-start.1) | collective-permute-done | bytes 655392 | tf_op jit(solution)/shard_map/ppermute | solution.py:199
  22.7 0.1 slice_add_fusion.2
  22.8 3.3 %collective-permute-start.2 = (f32[4,40,512]{2,1,0:T(8,128)S(1)}, f32[4,40,512]{2,1,0:T(8,128)S(1)}, u32[]{:S(2)}, u32[]{:S(2)}) collective-permute-start(f32[4,40,512]{2,1,0:T(8,128)S(1)} %slice_add_fusion.2), channel_id=1, source_target_pairs={{0,16},{1,17},{2,18},{3,19},{4,12},{5,13},{6,14},{7,15},{8,24},{9,... | collective-permute-start | bytes 983048 | tf_op jit(solution)/shard_map/ppermute | solution.py:199
  26.2 0.0 collective-permute-done.6
  26.2 3.5 %collective-permute-start.7 = (f32[4,24,512]{2,1,0:T(8,128)S(1)}, f32[4,24,512]{2,1,0:T(8,128)S(1)}, u32[]{:S(2)}, u32[]{:S(2)}) collective-permute-start(f32[4,24,512]{2,1,0:T(8,128)S(1)} %slice_add_fusion.4), channel_id=1, source_target_pairs={{0,1},{1,0},{2,3},{3,2},{4,6},{5,7},{6,4},{7,5},{8,9},{9,8},{10,11... | collective-permute-start | bytes 589832 | tf_op jit(solution)/shard_map/ppermute | solution.py:199
  29.7 1.5 %collective-permute-done.2 = f32[4,40,512]{2,1,0:T(8,128)S(1)} collective-permute-done((f32[4,40,512]{2,1,0:T(8,128)S(1)}, f32[4,40,512]{2,1,0:T(8,128)S(1)}, u32[]{:S(2)}, u32[]{:S(2)}) %collective-permute-start.2) | collective-permute-done | bytes 327712 | tf_op jit(solution)/shard_map/ppermute | solution.py:199
  31.3 0.0 copy-start
  31.3 2.2 %collective-permute-start.3 = (f32[2,40,512]{2,1,0:T(8,128)S(1)}, f32[2,40,512]{2,1,0:T(8,128)S(1)}, u32[]{:S(2)}, u32[]{:S(2)}) collective-permute-start(f32[2,40,512]{2,1,0:T(8,128)S(1)} %slice_add_fusion.6), channel_id=1, source_target_pairs={{0,1},{1,0},{2,3},{3,2},{4,5},{5,4},{6,7},{7,6},{8,9},{9,8},{10,11... | collective-permute-start | bytes 491528 | tf_op jit(solution)/shard_map/ppermute | solution.py:199
  33.4 2.4 %collective-permute-done.7 = f32[4,24,512]{2,1,0:T(8,128)S(1)} collective-permute-done((f32[4,24,512]{2,1,0:T(8,128)S(1)}, f32[4,24,512]{2,1,0:T(8,128)S(1)}, u32[]{:S(2)}, u32[]{:S(2)}) %collective-permute-start.7) | collective-permute-done | bytes 196640 | tf_op jit(solution)/shard_map/ppermute | solution.py:199
  35.8 0.5 collective-permute-start.8
  36.3 2.3 %collective-permute-done.3 = f32[2,40,512]{2,1,0:T(8,128)S(1)} collective-permute-done((f32[2,40,512]{2,1,0:T(8,128)S(1)}, f32[2,40,512]{2,1,0:T(8,128)S(1)}, u32[]{:S(2)}, u32[]{:S(2)}) %collective-permute-start.3) | collective-permute-done | bytes 163872 | tf_op jit(solution)/shard_map/ppermute | solution.py:199
  38.7 0.1 slice_add_fusion.12
  38.7 1.5 %collective-permute-start.4 = (f32[1,40,512]{2,1,0:T(8,128)S(1)}, f32[1,40,512]{2,1,0:T(8,128)S(1)}, u32[]{:S(2)}, u32[]{:S(2)}) collective-permute-start(f32[1,40,512]{2,1,0:T(8,128)S(1)} %get-tuple-element.23), channel_id=1, source_target_pairs={{0,2},{1,3},{2,0},{3,1},{4,6},{5,7},{6,4},{7,5},{8,10},{9,11},{10,... | collective-permute-start | bytes 245768 | tf_op jit(solution)/shard_map/ppermute | solution.py:199
  40.2 0.3 collective-permute-done.8
  40.6 1.5 %collective-permute-start.9 = (f32[1,24,512]{2,1,0:T(8,128)S(1)}, f32[1,24,512]{2,1,0:T(8,128)S(1)}, u32[]{:S(2)}, u32[]{:S(2)}) collective-permute-start(f32[1,24,512]{2,1,0:T(8,128)S(1)} %get-tuple-element.26), channel_id=1, source_target_pairs={{0,16},{1,17},{2,18},{3,19},{4,12},{5,13},{6,14},{7,15},{8,24},{9,... | collective-permute-start | bytes 147464 | tf_op jit(solution)/shard_map/ppermute | solution.py:199
  42.1 2.7 %collective-permute-done.9 = f32[1,24,512]{2,1,0:T(8,128)S(1)} collective-permute-done((f32[1,24,512]{2,1,0:T(8,128)S(1)}, f32[1,24,512]{2,1,0:T(8,128)S(1)}, u32[]{:S(2)}, u32[]{:S(2)}) %collective-permute-start.9) | collective-permute-done | bytes 49184 | tf_op jit(solution)/shard_map/ppermute | solution.py:199
  44.7 0.4 collective-permute-done.4
  45.1 0.0 copy-done
  45.1 0.9 %stats.1 = (f32[1,64,512]{2,1,0:T(8,128)}, f32[64,512]{1,0:T(8,128)S(1)}, f32[64,512]{1,0:T(8,128)S(1)}, f32[32,128]{1,0:T(8,128)S(1)}) custom-call(f32[1,512,512]{2,1,0:T(8,128)S(1)} %copy-done, f32[40,512]{1,0:T(8,128)S(1)} %get-tuple-element.24.rest_0_, f32[40,512]{1,0:T(8,128)S(1)} %get-tuple-element.25.rest_1_, ...), custom_call_target="tpu_custom_call" | custom-call | tf_op jit(solution)/shard_map/stats/pallas_call | solution.py:223
  46.0 12.6 %all_to_all.11 = f32[32,1,128]{2,1,0:T(1,128)S(1)} all-to-all(f32[32,1,128]{2,1,0:T(1,128)S(1)} %bitcast.32), channel_id=1, replica_groups=mesh['ops'=8,'sec'=4] {'ops','sec'}, dimensions={0} | all-to-all | bytes 32768 | tf_op jit(solution)/shard_map/all_to_all | solution.py:237
  58.6 1.3 %finish.1 = (f32[1,64,512]{2,1,0:T(8,128)}, f32[2]{0:T(128)}) custom-call(f32[64,512]{1,0:T(8,128)S(1)} %get-tuple-element.18.psi_ref, f32[64,512]{1,0:T(8,128)S(1)} %get-tuple-element.19.sigma_ref, f32[32,128]{1,0:T(8,128)S(1)} %bitcast.30), custom_call_target="tpu_custom_call" | custom-call | tf_op jit(solution)/shard_map/finish/pallas_call | solution.py:238
  (4 shorter events, 0.2 us)
Async XLA Ops:
  6.2 3.1 %collective-permute-start = (f32[16,40,512]{2,1,0:T(8,128)S(1)}, f32[16,40,512]{2,1,0:T(8,128)S(1)}, u32[]{:S(2)}, u32[]{:S(2)}) collective-permute-start(f32[16,40,512]{2,1,0:T(8,128)S(1)} %get-tuple-element.14), channel_id=1, source_target_pairs={{0,4},{4,0},{8,12},{12,8},{16,20},{20,16},{24,28},{28,24},{1,5},{5... | collective-permute-start | bytes 3932168 | tf_op jit(solution)/shard_map/ppermute | solution.py:215
  6.7 7.5 %collective-permute-start.5 = (f32[16,24,512]{2,1,0:T(8,128)S(1)}, f32[16,24,512]{2,1,0:T(8,128)S(1)}, u32[]{:S(2)}, u32[]{:S(2)}) collective-permute-start(f32[16,24,512]{2,1,0:T(8,128)S(1)} %get-tuple-element.16), channel_id=1, source_target_pairs={{0,4},{4,0},{8,12},{12,8},{16,20},{20,16},{24,28},{28,24},{1,5},{5... | collective-permute-start | bytes 2359304 | tf_op jit(solution)/shard_map/ppermute | solution.py:216
  9.5 13.3 %collective-permute-start.1 = (f32[8,40,512]{2,1,0:T(8,128)S(1)}, f32[8,40,512]{2,1,0:T(8,128)S(1)}, u32[]{:S(2)}, u32[]{:S(2)}) collective-permute-start(f32[8,40,512]{2,1,0:T(8,128)S(1)} %slice_add_fusion), channel_id=1, source_target_pairs={{0,8},{1,9},{2,10},{3,11},{4,20},{5,21},{6,22},{7,23},{8,0},{9,1},... | collective-permute-start | bytes 1966088 | tf_op jit(solution)/shard_map/ppermute | solution.py:199
  14.2 11.9 %collective-permute-start.6 = (f32[8,24,512]{2,1,0:T(8,128)S(1)}, f32[8,24,512]{2,1,0:T(8,128)S(1)}, u32[]{:S(2)}, u32[]{:S(2)}) collective-permute-start(f32[8,24,512]{2,1,0:T(8,128)S(1)} %slice_add_fusion.1), channel_id=1, source_target_pairs={{0,2},{1,3},{2,0},{3,1},{4,5},{5,4},{6,7},{7,6},{8,10},{9,11},{10,... | collective-permute-start | bytes 1179656 | tf_op jit(solution)/shard_map/ppermute | solution.py:199
  22.8 8.4 %collective-permute-start.2 = (f32[4,40,512]{2,1,0:T(8,128)S(1)}, f32[4,40,512]{2,1,0:T(8,128)S(1)}, u32[]{:S(2)}, u32[]{:S(2)}) collective-permute-start(f32[4,40,512]{2,1,0:T(8,128)S(1)} %slice_add_fusion.2), channel_id=1, source_target_pairs={{0,16},{1,17},{2,18},{3,19},{4,12},{5,13},{6,14},{7,15},{8,24},{9,... | collective-permute-start | bytes 983048 | tf_op jit(solution)/shard_map/ppermute | solution.py:199
  26.2 9.6 %collective-permute-start.7 = (f32[4,24,512]{2,1,0:T(8,128)S(1)}, f32[4,24,512]{2,1,0:T(8,128)S(1)}, u32[]{:S(2)}, u32[]{:S(2)}) collective-permute-start(f32[4,24,512]{2,1,0:T(8,128)S(1)} %slice_add_fusion.4), channel_id=1, source_target_pairs={{0,1},{1,0},{2,3},{3,2},{4,6},{5,7},{6,4},{7,5},{8,9},{9,8},{10,11... | collective-permute-start | bytes 589832 | tf_op jit(solution)/shard_map/ppermute | solution.py:199
  31.3 13.8 %copy-start = (f32[1,512,512]{2,1,0:T(8,128)S(1)}, f32[1,512,512]{2,1,0:T(8,128)}, u32[]{:S(2)}) copy-start(f32[1,512,512]{2,1,0:T(8,128)} %psi_ref.3) | copy-start | bytes 3145732
  31.3 7.4 %collective-permute-start.3 = (f32[2,40,512]{2,1,0:T(8,128)S(1)}, f32[2,40,512]{2,1,0:T(8,128)S(1)}, u32[]{:S(2)}, u32[]{:S(2)}) collective-permute-start(f32[2,40,512]{2,1,0:T(8,128)S(1)} %slice_add_fusion.6), channel_id=1, source_target_pairs={{0,1},{1,0},{2,3},{3,2},{4,5},{5,4},{6,7},{7,6},{8,9},{9,8},{10,11... | collective-permute-start | bytes 491528 | tf_op jit(solution)/shard_map/ppermute | solution.py:199
  35.8 4.7 %collective-permute-start.8 = (f32[2,24,512]{2,1,0:T(8,128)S(1)}, f32[2,24,512]{2,1,0:T(8,128)S(1)}, u32[]{:S(2)}, u32[]{:S(2)}) collective-permute-start(f32[2,24,512]{2,1,0:T(8,128)S(1)} %slice_add_fusion.9), channel_id=1, source_target_pairs={{0,8},{1,9},{2,10},{3,11},{4,20},{5,21},{6,22},{7,23},{8,0},{9,1},... | collective-permute-start | bytes 294920 | tf_op jit(solution)/shard_map/ppermute | solution.py:199
  38.7 6.4 %collective-permute-start.4 = (f32[1,40,512]{2,1,0:T(8,128)S(1)}, f32[1,40,512]{2,1,0:T(8,128)S(1)}, u32[]{:S(2)}, u32[]{:S(2)}) collective-permute-start(f32[1,40,512]{2,1,0:T(8,128)S(1)} %get-tuple-element.23), channel_id=1, source_target_pairs={{0,2},{1,3},{2,0},{3,1},{4,6},{5,7},{6,4},{7,5},{8,10},{9,11},{10,... | collective-permute-start | bytes 245768 | tf_op jit(solution)/shard_map/ppermute | solution.py:199
  40.6 4.2 %collective-permute-start.9 = (f32[1,24,512]{2,1,0:T(8,128)S(1)}, f32[1,24,512]{2,1,0:T(8,128)S(1)}, u32[]{:S(2)}, u32[]{:S(2)}) collective-permute-start(f32[1,24,512]{2,1,0:T(8,128)S(1)} %get-tuple-element.26), channel_id=1, source_target_pairs={{0,16},{1,17},{2,18},{3,19},{4,12},{5,13},{6,14},{7,15},{8,24},{9,... | collective-permute-start | bytes 147464 | tf_op jit(solution)/shard_map/ppermute | solution.py:199

commit v4 on v3

--- a/solution.py
+++ b/solution.py
@@ -27,7 +27,7 @@
     sector = [("sec", bit) for bit in range(sec_bits)]
     return (
         (plane + sector, turned + sector),
-        (sector[::-1] + plane, sector + turned),
+        (sector[::-1] + plane, sector + plane),
     )
 
 
@@ -57,7 +57,8 @@
 
 
 def sigma_kernel(orders, sectors, pieces, links_ref, psi_ref, lefts_ref, rights_ref, *rest):
-    outs, (psi, lefts, rights, psi_high, psi_low, targets, sems) = rest[:4], rest[4:]
+    outs, (psi, lefts, rights, psi_high, psi_low, targets, sems) = rest[:6], rest[6:]
+    stream_refs = ((outs[0:2], outs[2:4]), (outs[4:5], outs[5:6]))
     pairs, _, rows, states = lefts.shape
     blocks = lefts.shape[1] // 2
     me = lax.axis_index("ops")
@@ -102,7 +103,22 @@
                         slot_part(orders[stream][0], "ops", block << 1),
                         slot_part(orders[stream][1], "ops", block << 1),
                     )
-                    outs[2 * stream + away][block_part + sector_part] += product[away, block, start : start + piece]
+                    slot = block_part + sector_part
+                    term = product[away, block, start : start + piece]
+                    refs = stream_refs[stream][away]
+                    if len(refs) == 1:
+                        refs[0][slot] += term
+                        continue
+                    half = refs[0].shape[0]
+
+                    @pl.when(slot < half)
+                    def _():
+                        refs[0][slot] += term
+
+                    @pl.when(slot >= half)
+                    def _():
+                        refs[1][slot - half] += term
+
             start += piece
 
     for p in range(pairs):
@@ -117,9 +133,9 @@
 
 def partial_sigma(psi, lefts, rights, links, pieces, orders, sectors):
     pairs, owners, rows, states = lefts.shape
-    outs = [
-        jax.ShapeDtypeStruct((owners // 2 * sectors, piece, states), jnp.float32) for piece in pieces for _ in range(2)
-    ]
+    slots = owners // 2 * sectors
+    outs = [jax.ShapeDtypeStruct((slots // 2, pieces[0], states), jnp.float32)] * 4
+    outs += [jax.ShapeDtypeStruct((slots, pieces[1], states), jnp.float32)] * 2
     return pl.pallas_call(
         functools.partial(sigma_kernel, orders, sectors, pieces),
         in_specs=[pl.BlockSpec(memory_space=pltpu.HBM)] * 4,
@@ -186,18 +202,28 @@
     direction_ref[0] = (sigma_ref[...] - theta * psi_ref[...]) / norm
 
 
-def halve(parts, orders, ops_width, sectors):
-    for step in range(len(orders[0])):
-        partner = []
-        for ops in range(ops_width):
-            axis, bit = orders[ops & 1][step]
-            for sec in range(sectors):
-                to = (ops ^ (1 << bit), sec) if axis == "ops" else (ops, sec ^ (1 << bit))
-                partner.append((ops * sectors + sec, to[0] * sectors + to[1]))
-        half = parts[0].shape[0] // 2
-        leaving = sum(p[half:] for p in parts)
-        parts = [p[:half] for p in parts] + [lax.ppermute(leaving, ("ops", "sec"), partner)]
-    return [p[0] for p in parts]
+def after(value, earlier):
+    return lax.optimization_barrier((value, earlier))[0]
+
+
+def halving_step(leaving, orders, step, ops_width, sectors):
+    partner = []
+    for ops in range(ops_width):
+        axis, bit = orders[ops & 1][step]
+        for sec in range(sectors):
+            to = (ops ^ (1 << bit), sec) if axis == "ops" else (ops, sec ^ (1 << bit))
+            partner.append((ops * sectors + sec, to[0] * sectors + to[1]))
+    return lax.ppermute(leaving, ("ops", "sec"), partner)
+
+
+def leaving_of(parts):
+    half = parts[0].shape[0] // 2
+    return sum(p[half:] for p in parts)
+
+
+def staying_of(parts):
+    half = parts[0].shape[0] // 2
+    return [p[:half] for p in parts]
 
 
 def local(psi, left_ops, right_ops, links):
@@ -210,13 +236,25 @@
     links = links.reshape(pairs)
     orders = halving_orders(log2(ops_width), log2(sectors))
     pieces = (STREAM_P, rows - STREAM_P) if rows > STREAM_P else (rows // 2, rows - rows // 2)
-    keep_p, send_p, keep_q, send_q = partial_sigma(psi, lefts, rights, links, pieces, orders, sectors)
+    keep_low, keep_high, send_low, send_high, keep_q, send_q = partial_sigma(
+        psi, lefts, rights, links, pieces, orders, sectors
+    )
     swap = [(i, i ^ 1) for i in range(ops_width)]
-    came_p = lax.ppermute(send_p, "ops", swap)
-    came_q = lax.ppermute(send_q, "ops", swap)
-    stream_p = halve([keep_p, came_p], orders[0], ops_width, sectors)
-    stream_q = halve([keep_q, came_q], orders[1], ops_width, sectors)
-    terms = stream_p + stream_q
+    came_high, came_low, came_q = [lax.ppermute(x, "ops", swap) for x in (send_high, send_low, send_q)]
+    parts_q = [keep_q, came_q]
+    leaving_p, stream_p = keep_high + came_high, [keep_low, came_low]
+    leaving_q, stream_q = leaving_of(parts_q), staying_of(parts_q)
+    for step in range(len(orders[0][0])):
+        if step:
+            before = leaving_q
+            leaving_p, stream_p = leaving_of(stream_p), staying_of(stream_p)
+            leaving_q, stream_q = leaving_of(stream_q), staying_of(stream_q)
+            leaving_q = after(leaving_q, leaving_p)
+            if step > 1:
+                leaving_p = after(leaving_p, before)
+        stream_p = stream_p + [halving_step(leaving_p, orders[0], step, ops_width, sectors)]
+        stream_q = stream_q + [halving_step(leaving_q, orders[1], step, ops_width, sectors)]
+    terms = [p[0] for p in stream_p + stream_q]
     groups = [len(stream_p), len(stream_q)]
     devices = ops_width * sectors
     vmem = pl.BlockSpec(memory_space=pltpu.VMEM)

time: 59.7 us -> 58.3 us (0.977)
  waiting for transfers between devices: 17.9 us -> 13.8 us
  Pallas kernels: 7.73 us -> 10.5 us
  blocking collectives: 12.6 us -> 10.7 us
  starting transfers between devices: 20.4 us -> 21.7 us
    ppermute x10 -> x11, waiting for transfers between devices: 17.9 us -> 13.8 us  [the longest x8 12.3 us: halving_step(): return lax.ppermute(leaving, ('ops', 'sec'), partner)]
    pallas_call x1, Pallas kernels: 5.58 us -> 8.34 us  [partial_sigma(): pl.pallas_call(functools.partial(sigma_kernel, orders, sectors, pieces),...]
    all_to_all x1, blocking collectives: 12.6 us -> 10.7 us  [local(): stats = lax.all_to_all(stats, ('ops', 'sec'), 0, 0, tiled=True)]
    ppermute x10 -> x11, starting transfers between devices: 20.4 us -> 21.7 us  [the longest x8 21.1 us: halving_step(): return lax.ppermute(leaving, ('ops', 'sec'), partner)]
  transfers between devices with their start and end apart: 10 -> 11, of which waited for: 8 -> 7; matrix products, arithmetic and copies ran while one was open for 1% -> 1% of each run, Pallas kernels for 0% -> 0%
where the time goes in v4:
time: 58.3 us; the launch traced here: 57.9 us
  starting transfers between devices  21.7 us (37%)
  waiting for transfers between devices  13.8 us (24%)
  blocking collectives  10.7 us (18%)
  Pallas kernels  10.5 us (18%)
  between operations  0.69 us (1%)
    ppermute x8, starting transfers between devices, halving_step(): return lax.ppermute(leaving, ('ops', 'sec'), partner)  21.1 us
    ppermute x8, waiting for transfers between devices, halving_step(): return lax.ppermute(leaving, ('ops', 'sec'), partner)  12.3 us
    all_to_all x1, blocking collectives, local(): stats = lax.all_to_all(stats, ('ops', 'sec'), 0, 0, tiled=True)  10.7 us
    pallas_call x1, Pallas kernels, partial_sigma(): pl.pallas_call(functools.partial(sigma_kernel, orders, sectors, pieces),...  8.34 us
    ppermute x3, waiting for transfers between devices, local(): lax.ppermute(x, 'ops', swap)  1.51 us
    pallas_call x1, Pallas kernels, local(): pl.pallas_call(finish_kernel, in_specs=[vmem] * 3, out_specs=[vmem, pl.Bl...  1.28 us
  transfers between devices with their start and end apart: 11, of which 7 were waited for; matrix products, arithmetic and copies ran while one was open for 1% of the time, Pallas kernels for 0%

profile of v4, /device:TPU:0, one launch (start us, length us, event | category | flops | bytes accessed | tf_op | source)
XLA Modules:
  0.0 57.9 jit_solution(11749605904979089262)
XLA Ops:
  0.6 8.3 %partial_sigma.1 = (f32[8,40,512]{2,1,0:T(8,128)S(1)}, f32[8,40,512]{2,1,0:T(8,128)S(1)}, f32[8,40,512]{2,1,0:T(8,128)S(1)}, f32[8,40,512]{2,1,0:T(8,128)S(1)}, ...) custom-call(s32[4]{0:T(128)} %bitcast.35, f32[1,512,512]{2,1,0:T(8,128)} %psi_ref.3, f32[4,8,64,512]{3,2,1,0:T(8,128)} %bitcast.33, ...), custom_call_target="tpu_custom_call" | custom-call | flops 6442450944 | bytes 9437184 | tf_op jit(solution)/shard_map/partial_sigma/pallas_call | solution.py:139
  9.0 0.1 collective-permute-start.1
  9.1 0.5 collective-permute-start.4
  9.6 0.1 collective-permute-start
  9.6 1.5 %collective-permute-done.1 = f32[8,40,512]{2,1,0:T(8,128)S(1)} collective-permute-done((f32[8,40,512]{2,1,0:T(8,128)S(1)}, f32[8,40,512]{2,1,0:T(8,128)S(1)}, u32[]{:S(2)}, u32[]{:S(2)}) %collective-permute-start.1) | collective-permute-done | bytes 655392 | tf_op jit(solution)/shard_map/ppermute | solution.py:243
  11.1 0.1 add.60
  11.3 2.4 %collective-permute-start.2 = (f32[8,40,512]{2,1,0:T(8,128)S(1)}, f32[8,40,512]{2,1,0:T(8,128)S(1)}, u32[]{:S(2)}, u32[]{:S(2)}) collective-permute-start(f32[8,40,512]{2,1,0:T(8,128)S(1)} %add.60), channel_id=1, source_target_pairs={{0,8},{1,9},{2,10},{3,11},{4,20},{5,21},{6,22},{7,23},{8,0},{9,1},... | collective-permute-start | bytes 1966088 | tf_op jit(solution)/shard_map/ppermute | solution.py:216
  13.6 0.0 collective-permute-done.4
  13.6 0.1 slice_add_fusion
  13.7 4.0 %collective-permute-start.5 = (f32[8,24,512]{2,1,0:T(8,128)S(1)}, f32[8,24,512]{2,1,0:T(8,128)S(1)}, u32[]{:S(2)}, u32[]{:S(2)}) collective-permute-start(f32[8,24,512]{2,1,0:T(8,128)S(1)} %slice_add_fusion), channel_id=1, source_target_pairs={{0,2},{1,3},{2,0},{3,1},{4,5},{5,4},{6,7},{7,6},{8,10},{9,11},{10,... | collective-permute-start | bytes 1179656 | tf_op jit(solution)/shard_map/ppermute | solution.py:216
  17.7 0.0 collective-permute-done
  17.7 4.5 %collective-permute-done.2 = f32[8,40,512]{2,1,0:T(8,128)S(1)} collective-permute-done((f32[8,40,512]{2,1,0:T(8,128)S(1)}, f32[8,40,512]{2,1,0:T(8,128)S(1)}, u32[]{:S(2)}, u32[]{:S(2)}) %collective-permute-start.2) | collective-permute-done | bytes 655392 | tf_op jit(solution)/shard_map/ppermute | solution.py:216
  22.2 0.1 slice_add_fusion.1
  22.3 2.2 %collective-permute-start.3 = (f32[4,40,512]{2,1,0:T(8,128)S(1)}, f32[4,40,512]{2,1,0:T(8,128)S(1)}, u32[]{:S(2)}, u32[]{:S(2)}) collective-permute-start(f32[4,40,512]{2,1,0:T(8,128)S(1)} %slice_add_fusion.1), channel_id=1, source_target_pairs={{0,16},{1,17},{2,18},{3,19},{4,12},{5,13},{6,14},{7,15},{8,24},{9,... | collective-permute-start | bytes 983048 | tf_op jit(solution)/shard_map/ppermute | solution.py:216
  24.5 2.0 %collective-permute-done.5 = f32[8,24,512]{2,1,0:T(8,128)S(1)} collective-permute-done((f32[8,24,512]{2,1,0:T(8,128)S(1)}, f32[8,24,512]{2,1,0:T(8,128)S(1)}, u32[]{:S(2)}, u32[]{:S(2)}) %collective-permute-start.5) | collective-permute-done | bytes 393248 | tf_op jit(solution)/shard_map/ppermute | solution.py:216
  26.5 2.5 %collective-permute-start.7 = (f32[4,24,512]{2,1,0:T(8,128)S(1)}, f32[4,24,512]{2,1,0:T(8,128)S(1)}, u32[]{:S(2)}, u32[]{:S(2)}) collective-permute-start(f32[4,24,512]{2,1,0:T(8,128)S(1)} %slice_add_fusion.3), channel_id=1, source_target_pairs={{0,1},{1,0},{2,3},{3,2},{4,6},{5,7},{6,4},{7,5},{8,9},{9,8},{10,11... | collective-permute-start | bytes 589832 | tf_op jit(solution)/shard_map/ppermute | solution.py:216
  29.0 0.5 collective-permute-done.3
  29.5 0.1 slice_add_fusion.5
  29.6 2.9 %collective-permute-start.6 = (f32[2,40,512]{2,1,0:T(8,128)S(1)}, f32[2,40,512]{2,1,0:T(8,128)S(1)}, u32[]{:S(2)}, u32[]{:S(2)}) collective-permute-start(f32[2,40,512]{2,1,0:T(8,128)S(1)} %slice_add_fusion.5), channel_id=1, source_target_pairs={{0,1},{1,0},{2,3},{3,2},{4,5},{5,4},{6,7},{7,6},{8,9},{9,8},{10,11... | collective-permute-start | bytes 491528 | tf_op jit(solution)/shard_map/ppermute | solution.py:216
  32.5 2.2 %collective-permute-done.7 = f32[4,24,512]{2,1,0:T(8,128)S(1)} collective-permute-done((f32[4,24,512]{2,1,0:T(8,128)S(1)}, f32[4,24,512]{2,1,0:T(8,128)S(1)}, u32[]{:S(2)}, u32[]{:S(2)}) %collective-permute-start.7) | collective-permute-done | bytes 196640 | tf_op jit(solution)/shard_map/ppermute | solution.py:216
  34.7 3.6 %collective-permute-start.9 = (f32[2,24,512]{2,1,0:T(8,128)S(1)}, f32[2,24,512]{2,1,0:T(8,128)S(1)}, u32[]{:S(2)}, u32[]{:S(2)}) collective-permute-start(f32[2,24,512]{2,1,0:T(8,128)S(1)} %slice_add_fusion.8), channel_id=1, source_target_pairs={{0,8},{1,9},{2,10},{3,11},{4,12},{5,13},{6,14},{7,15},{8,0},{9,1},... | collective-permute-start | bytes 294920 | tf_op jit(solution)/shard_map/ppermute | solution.py:216
  38.3 0.0 collective-permute-done.6
  38.3 0.1 slice_add_fusion.11
  38.3 1.7 %collective-permute-start.8 = (f32[1,40,512]{2,1,0:T(8,128)S(1)}, f32[1,40,512]{2,1,0:T(8,128)S(1)}, u32[]{:S(2)}, u32[]{:S(2)}) collective-permute-start(f32[1,40,512]{2,1,0:T(8,128)S(1)} %get-tuple-element.29), channel_id=1, source_target_pairs={{0,2},{1,3},{2,0},{3,1},{4,6},{5,7},{6,4},{7,5},{8,10},{9,11},{10,... | collective-permute-start | bytes 245768 | tf_op jit(solution)/shard_map/ppermute | solution.py:216
  40.0 0.8 %collective-permute-done.9 = f32[2,24,512]{2,1,0:T(8,128)S(1)} collective-permute-done((f32[2,24,512]{2,1,0:T(8,128)S(1)}, f32[2,24,512]{2,1,0:T(8,128)S(1)}, u32[]{:S(2)}, u32[]{:S(2)}) %collective-permute-start.9) | collective-permute-done | bytes 98336 | tf_op jit(solution)/shard_map/ppermute | solution.py:216
  40.9 1.9 %collective-permute-start.10 = (f32[1,24,512]{2,1,0:T(8,128)S(1)}, f32[1,24,512]{2,1,0:T(8,128)S(1)}, u32[]{:S(2)}, u32[]{:S(2)}) collective-permute-start(f32[1,24,512]{2,1,0:T(8,128)S(1)} %get-tuple-element.30), channel_id=1, source_target_pairs={{0,16},{1,17},{2,18},{3,19},{4,20},{5,21},{6,22},{7,23},{8,24},{9,... | collective-permute-start | bytes 147464 | tf_op jit(solution)/shard_map/ppermute | solution.py:216
  42.8 2.3 %collective-permute-done.10 = f32[1,24,512]{2,1,0:T(8,128)S(1)} collective-permute-done((f32[1,24,512]{2,1,0:T(8,128)S(1)}, f32[1,24,512]{2,1,0:T(8,128)S(1)}, u32[]{:S(2)}, u32[]{:S(2)}) %collective-permute-start.10) | collective-permute-done | bytes 49184 | tf_op jit(solution)/shard_map/ppermute | solution.py:216
  45.1 0.0 collective-permute-done.8
  45.1 0.0 copy-done
  45.1 0.9 %stats.1 = (f32[1,64,512]{2,1,0:T(8,128)}, f32[64,512]{1,0:T(8,128)S(1)}, f32[64,512]{1,0:T(8,128)S(1)}, f32[32,128]{1,0:T(8,128)S(1)}) custom-call(f32[1,512,512]{2,1,0:T(8,128)S(1)} %copy-done, f32[40,512]{1,0:T(8,128)S(1)} %get-tuple-element.41.rest_0_, f32[40,512]{1,0:T(8,128)S(1)} %get-tuple-element.42.rest_1_, ...), custom_call_target="tpu_custom_call" | custom-call | tf_op jit(solution)/shard_map/stats/pallas_call | solution.py:261
  46.0 10.7 %all_to_all.11 = f32[32,1,128]{2,1,0:T(1,128)S(1)} all-to-all(f32[32,1,128]{2,1,0:T(1,128)S(1)} %bitcast.32), channel_id=1, replica_groups=mesh['ops'=8,'sec'=4] {'ops','sec'}, dimensions={0} | all-to-all | bytes 32768 | tf_op jit(solution)/shard_map/all_to_all | solution.py:275
  56.7 1.3 %finish.1 = (f32[1,64,512]{2,1,0:T(8,128)}, f32[2]{0:T(128)}) custom-call(f32[64,512]{1,0:T(8,128)S(1)} %get-tuple-element.32.psi_ref, f32[64,512]{1,0:T(8,128)S(1)} %get-tuple-element.33.sigma_ref, f32[32,128]{1,0:T(8,128)S(1)} %bitcast.30), custom_call_target="tpu_custom_call" | custom-call | tf_op jit(solution)/shard_map/finish/pallas_call | solution.py:276
  (4 shorter events, 0.1 us)
Async XLA Ops:
  9.0 2.2 %collective-permute-start.1 = (f32[8,40,512]{2,1,0:T(8,128)S(1)}, f32[8,40,512]{2,1,0:T(8,128)S(1)}, u32[]{:S(2)}, u32[]{:S(2)}) collective-permute-start(f32[8,40,512]{2,1,0:T(8,128)S(1)} %get-tuple-element.23), channel_id=1, source_target_pairs={{0,4},{4,0},{8,12},{12,8},{16,20},{20,16},{24,28},{28,24},{1,5},{5... | collective-permute-start | bytes 1966088 | tf_op jit(solution)/shard_map/ppermute | solution.py:243
  9.1 4.6 %collective-permute-start.4 = (f32[16,24,512]{2,1,0:T(8,128)S(1)}, f32[16,24,512]{2,1,0:T(8,128)S(1)}, u32[]{:S(2)}, u32[]{:S(2)}) collective-permute-start(f32[16,24,512]{2,1,0:T(8,128)S(1)} %get-tuple-element.25), channel_id=1, source_target_pairs={{0,4},{4,0},{8,12},{12,8},{16,20},{20,16},{24,28},{28,24},{1,5},{5... | collective-permute-start | bytes 2359304 | tf_op jit(solution)/shard_map/ppermute | solution.py:243
  9.6 8.2 %collective-permute-start = (f32[8,40,512]{2,1,0:T(8,128)S(1)}, f32[8,40,512]{2,1,0:T(8,128)S(1)}, u32[]{:S(2)}, u32[]{:S(2)}) collective-permute-start(f32[8,40,512]{2,1,0:T(8,128)S(1)} %get-tuple-element.21), channel_id=1, source_target_pairs={{0,4},{4,0},{8,12},{12,8},{16,20},{20,16},{24,28},{28,24},{1,5},{5... | collective-permute-start | bytes 1966088 | tf_op jit(solution)/shard_map/ppermute | solution.py:243
  11.1 33.9 %copy-start = (f32[1,512,512]{2,1,0:T(8,128)S(1)}, f32[1,512,512]{2,1,0:T(8,128)}, u32[]{:S(2)}) copy-start(f32[1,512,512]{2,1,0:T(8,128)} %psi_ref.3) | copy-start | bytes 3145732
  11.3 10.9 %collective-permute-start.2 = (f32[8,40,512]{2,1,0:T(8,128)S(1)}, f32[8,40,512]{2,1,0:T(8,128)S(1)}, u32[]{:S(2)}, u32[]{:S(2)}) collective-permute-start(f32[8,40,512]{2,1,0:T(8,128)S(1)} %add.60), channel_id=1, source_target_pairs={{0,8},{1,9},{2,10},{3,11},{4,20},{5,21},{6,22},{7,23},{8,0},{9,1},... | collective-permute-start | bytes 1966088 | tf_op jit(solution)/shard_map/ppermute | solution.py:216
  13.7 12.8 %collective-permute-start.5 = (f32[8,24,512]{2,1,0:T(8,128)S(1)}, f32[8,24,512]{2,1,0:T(8,128)S(1)}, u32[]{:S(2)}, u32[]{:S(2)}) collective-permute-start(f32[8,24,512]{2,1,0:T(8,128)S(1)} %slice_add_fusion), channel_id=1, source_target_pairs={{0,2},{1,3},{2,0},{3,1},{4,5},{5,4},{6,7},{7,6},{8,10},{9,11},{10,... | collective-permute-start | bytes 1179656 | tf_op jit(solution)/shard_map/ppermute | solution.py:216
  22.3 7.2 %collective-permute-start.3 = (f32[4,40,512]{2,1,0:T(8,128)S(1)}, f32[4,40,512]{2,1,0:T(8,128)S(1)}, u32[]{:S(2)}, u32[]{:S(2)}) collective-permute-start(f32[4,40,512]{2,1,0:T(8,128)S(1)} %slice_add_fusion.1), channel_id=1, source_target_pairs={{0,16},{1,17},{2,18},{3,19},{4,12},{5,13},{6,14},{7,15},{8,24},{9,... | collective-permute-start | bytes 983048 | tf_op jit(solution)/shard_map/ppermute | solution.py:216
  26.5 8.2 %collective-permute-start.7 = (f32[4,24,512]{2,1,0:T(8,128)S(1)}, f32[4,24,512]{2,1,0:T(8,128)S(1)}, u32[]{:S(2)}, u32[]{:S(2)}) collective-permute-start(f32[4,24,512]{2,1,0:T(8,128)S(1)} %slice_add_fusion.3), channel_id=1, source_target_pairs={{0,1},{1,0},{2,3},{3,2},{4,6},{5,7},{6,4},{7,5},{8,9},{9,8},{10,11... | collective-permute-start | bytes 589832 | tf_op jit(solution)/shard_map/ppermute | solution.py:216
  29.6 8.7 %collective-permute-start.6 = (f32[2,40,512]{2,1,0:T(8,128)S(1)}, f32[2,40,512]{2,1,0:T(8,128)S(1)}, u32[]{:S(2)}, u32[]{:S(2)}) collective-permute-start(f32[2,40,512]{2,1,0:T(8,128)S(1)} %slice_add_fusion.5), channel_id=1, source_target_pairs={{0,1},{1,0},{2,3},{3,2},{4,5},{5,4},{6,7},{7,6},{8,9},{9,8},{10,11... | collective-permute-start | bytes 491528 | tf_op jit(solution)/shard_map/ppermute | solution.py:216
  34.7 6.2 %collective-permute-start.9 = (f32[2,24,512]{2,1,0:T(8,128)S(1)}, f32[2,24,512]{2,1,0:T(8,128)S(1)}, u32[]{:S(2)}, u32[]{:S(2)}) collective-permute-start(f32[2,24,512]{2,1,0:T(8,128)S(1)} %slice_add_fusion.8), channel_id=1, source_target_pairs={{0,8},{1,9},{2,10},{3,11},{4,12},{5,13},{6,14},{7,15},{8,0},{9,1},... | collective-permute-start | bytes 294920 | tf_op jit(solution)/shard_map/ppermute | solution.py:216
  38.3 6.7 %collective-permute-start.8 = (f32[1,40,512]{2,1,0:T(8,128)S(1)}, f32[1,40,512]{2,1,0:T(8,128)S(1)}, u32[]{:S(2)}, u32[]{:S(2)}) collective-permute-start(f32[1,40,512]{2,1,0:T(8,128)S(1)} %get-tuple-element.29), channel_id=1, source_target_pairs={{0,2},{1,3},{2,0},{3,1},{4,6},{5,7},{6,4},{7,5},{8,10},{9,11},{10,... | collective-permute-start | bytes 245768 | tf_op jit(solution)/shard_map/ppermute | solution.py:216
  40.9 4.2 %collective-permute-start.10 = (f32[1,24,512]{2,1,0:T(8,128)S(1)}, f32[1,24,512]{2,1,0:T(8,128)S(1)}, u32[]{:S(2)}, u32[]{:S(2)}) collective-permute-start(f32[1,24,512]{2,1,0:T(8,128)S(1)} %get-tuple-element.30), channel_id=1, source_target_pairs={{0,16},{1,17},{2,18},{3,19},{4,20},{5,21},{6,22},{7,23},{8,24},{9,... | collective-permute-start | bytes 147464 | tf_op jit(solution)/shard_map/ppermute | solution.py:216

commit v5 on v4

--- a/solution.py
+++ b/solution.py
@@ -161,8 +161,8 @@
 
 
 def stats_kernel(groups, psi_ref, *rest):
-    ins, (sigma_ref, held_ref, psi_rows_ref, stats_ref, sem) = rest[:-5], rest[-5:]
-    rows = sigma_ref.shape[1]
+    ins, (held_ref, psi_rows_ref, stats_ref, sem) = rest[:-4], rest[-4:]
+    rows = held_ref.shape[0]
     copy = pltpu.make_async_copy(
         psi_ref.at[0, pl.ds(pl.multiple_of(lax.axis_index("ops") * rows, rows), rows)], psi_rows_ref, sem
     )
@@ -180,7 +180,6 @@
     copy.wait()
     psi = psi_rows_ref[...]
     sigma = held_ref[...]
-    sigma_ref[0] = sigma
     weight = jnp.sum(psi * psi)
     correlation = jnp.sum(psi * sigma)
     theta = jnp.where(weight > 0.0, correlation / weight, 0.0)
@@ -190,7 +189,8 @@
     stats_ref[...] = jnp.where(lane == 0, weight, jnp.where(lane == 1, theta, jnp.where(lane == 2, squared, 0.0)))
 
 
-def finish_kernel(psi_ref, sigma_ref, stats_ref, direction_ref, energies_ref):
+def finish_kernel(psi_ref, held_ref, stats_ref, sigma_ref, direction_ref, energies_ref):
+    sigma_ref[0] = held_ref[...]
     weights = stats_ref[:, 0:1]
     thetas = stats_ref[:, 1:2]
     squares = stats_ref[:, 2:3]
@@ -199,7 +199,7 @@
     norm = jnp.sqrt(jnp.sum(squares + weights * apart * apart))
     energies_ref[0] = theta
     energies_ref[1] = norm
-    direction_ref[0] = (sigma_ref[...] - theta * psi_ref[...]) / norm
+    direction_ref[0] = (held_ref[...] - theta * psi_ref[...]) / norm
 
 
 def after(value, earlier):
@@ -258,12 +258,11 @@
     groups = [len(stream_p), len(stream_q)]
     devices = ops_width * sectors
     vmem = pl.BlockSpec(memory_space=pltpu.VMEM)
-    sigma, held, psi_rows, stats = pl.pallas_call(
+    held, psi_rows, stats = pl.pallas_call(
         functools.partial(stats_kernel, groups),
         in_specs=[pl.BlockSpec(memory_space=pltpu.HBM)] + [vmem] * len(terms),
-        out_specs=[vmem] * 4,
+        out_specs=[vmem] * 3,
         out_shape=[
-            jax.ShapeDtypeStruct((1, rows, states), jnp.float32),
             jax.ShapeDtypeStruct((rows, states), jnp.float32),
             jax.ShapeDtypeStruct((rows, states), jnp.float32),
             jax.ShapeDtypeStruct((devices, 128), jnp.float32),
@@ -273,11 +272,12 @@
         name="stats",
     )(psi, *terms)
     stats = lax.all_to_all(stats, ("ops", "sec"), 0, 0, tiled=True)
-    direction, energies = pl.pallas_call(
+    sigma, direction, energies = pl.pallas_call(
         finish_kernel,
         in_specs=[vmem] * 3,
-        out_specs=[vmem, pl.BlockSpec(memory_space=pltpu.SMEM)],
+        out_specs=[vmem, vmem, pl.BlockSpec(memory_space=pltpu.SMEM)],
         out_shape=[
+            jax.ShapeDtypeStruct((1, rows, states), jnp.float32),
             jax.ShapeDtypeStruct((1, rows, states), jnp.float32),
             jax.ShapeDtypeStruct((2,), jnp.float32),
         ],

time: 58.3 us -> 59.1 us (1.014)
  waiting for transfers between devices: 13.8 us -> 25.2 us
  starting transfers between devices: 21.7 us -> 13.7 us
  Pallas kernels: 10.5 us -> 7.63 us
    ppermute x8, waiting for transfers between devices: 12.3 us -> 24 us  [halving_step(): return lax.ppermute(leaving, ('ops', 'sec'), partner)]
    ppermute x8, starting transfers between devices: 21.1 us -> 12.1 us  [halving_step(): return lax.ppermute(leaving, ('ops', 'sec'), partner)]
    pallas_call x1, Pallas kernels: 8.34 us -> 5.8 us  [partial_sigma(): pl.pallas_call(functools.partial(sigma_kernel, orders, sectors, pieces),...]
    ppermute x3, starting transfers between devices: 0.65 us -> 1.65 us  [local(): lax.ppermute(x, 'ops', swap)]
  transfers between devices with their start and end apart: 11 -> 11, of which waited for: 7 -> 8; matrix products, arithmetic and copies ran while one was open for 1% -> 1% of each run, Pallas kernels for 0% -> 0%
where the time goes in v5:
time: 59.1 us; the launch traced here: 58.3 us
  waiting for transfers between devices  25.2 us (43%)
  starting transfers between devices  13.7 us (23%)
  blocking collectives  10.6 us (18%)
  Pallas kernels  7.63 us (13%)
  between operations  0.69 us (1%)
    ppermute x8, waiting for transfers between devices, halving_step(): return lax.ppermute(leaving, ('ops', 'sec'), partner)  24 us
    ppermute x8, starting transfers between devices, halving_step(): return lax.ppermute(leaving, ('ops', 'sec'), partner)  12.1 us
    all_to_all x1, blocking collectives, local(): stats = lax.all_to_all(stats, ('ops', 'sec'), 0, 0, tiled=True)  10.6 us
    pallas_call x1, Pallas kernels, partial_sigma(): pl.pallas_call(functools.partial(sigma_kernel, orders, sectors, pieces),...  5.8 us
    ppermute x3, starting transfers between devices, local(): lax.ppermute(x, 'ops', swap)  1.65 us
    pallas_call x1, Pallas kernels, local(): pl.pallas_call(finish_kernel, in_specs=[vmem] * 3, out_specs=[vmem, vmem,...  1.28 us
    ppermute x3, waiting for transfers between devices, local(): lax.ppermute(x, 'ops', swap)  1.22 us
  transfers between devices with their start and end apart: 11, of which 8 were waited for; matrix products, arithmetic and copies ran while one was open for 1% of the time, Pallas kernels for 0%

profile of v5, /device:TPU:0, one launch (start us, length us, event | category | flops | bytes accessed | tf_op | source)
XLA Modules:
  0.0 58.3 jit_solution(6882912515761386290)
XLA Ops:
  0.6 5.8 %partial_sigma.1 = (f32[8,40,512]{2,1,0:T(8,128)S(1)}, f32[8,40,512]{2,1,0:T(8,128)S(1)}, f32[8,40,512]{2,1,0:T(8,128)S(1)}, f32[8,40,512]{2,1,0:T(8,128)S(1)}, ...) custom-call(s32[4]{0:T(128)} %bitcast.35, f32[1,512,512]{2,1,0:T(8,128)} %psi_ref.3, f32[4,8,64,512]{3,2,1,0:T(8,128)} %bitcast.33, ...), custom_call_target="tpu_custom_call" | custom-call | flops 6442450944 | bytes 9437184 | tf_op jit(solution)/shard_map/partial_sigma/pallas_call | solution.py:139
  6.4 1.1 %collective-permute-start.1 = (f32[8,40,512]{2,1,0:T(8,128)S(1)}, f32[8,40,512]{2,1,0:T(8,128)S(1)}, u32[]{:S(2)}, u32[]{:S(2)}) collective-permute-start(f32[8,40,512]{2,1,0:T(8,128)S(1)} %get-tuple-element.20), channel_id=1, source_target_pairs={{0,4},{4,0},{8,12},{12,8},{16,20},{20,16},{24,28},{28,24},{1,5},{5... | collective-permute-start | bytes 1966088 | tf_op jit(solution)/shard_map/ppermute | solution.py:243
  7.6 0.1 collective-permute-start.4
  7.7 0.4 collective-permute-start
  8.1 1.2 %collective-permute-done.1 = f32[8,40,512]{2,1,0:T(8,128)S(1)} collective-permute-done((f32[8,40,512]{2,1,0:T(8,128)S(1)}, f32[8,40,512]{2,1,0:T(8,128)S(1)}, u32[]{:S(2)}, u32[]{:S(2)}) %collective-permute-start.1) | collective-permute-done | bytes 655392 | tf_op jit(solution)/shard_map/ppermute | solution.py:243
  9.3 0.1 add.60
  9.4 6.1 %collective-permute-start.2 = (f32[8,40,512]{2,1,0:T(8,128)S(1)}, f32[8,40,512]{2,1,0:T(8,128)S(1)}, u32[]{:S(2)}, u32[]{:S(2)}) collective-permute-start(f32[8,40,512]{2,1,0:T(8,128)S(1)} %add.60), channel_id=1, source_target_pairs={{0,8},{1,9},{2,10},{3,11},{4,20},{5,21},{6,22},{7,23},{8,0},{9,1},... | collective-permute-start | bytes 1966088 | tf_op jit(solution)/shard_map/ppermute | solution.py:216
  15.5 0.0 collective-permute-done.4
  15.5 0.1 slice_add_fusion
  15.6 2.1 %collective-permute-start.5 = (f32[8,24,512]{2,1,0:T(8,128)S(1)}, f32[8,24,512]{2,1,0:T(8,128)S(1)}, u32[]{:S(2)}, u32[]{:S(2)}) collective-permute-start(f32[8,24,512]{2,1,0:T(8,128)S(1)} %slice_add_fusion), channel_id=1, source_target_pairs={{0,2},{1,3},{2,0},{3,1},{4,5},{5,4},{6,7},{7,6},{8,10},{9,11},{10,... | collective-permute-start | bytes 1179656 | tf_op jit(solution)/shard_map/ppermute | solution.py:216
  17.7 0.0 collective-permute-done
  17.7 6.4 %collective-permute-done.2 = f32[8,40,512]{2,1,0:T(8,128)S(1)} collective-permute-done((f32[8,40,512]{2,1,0:T(8,128)S(1)}, f32[8,40,512]{2,1,0:T(8,128)S(1)}, u32[]{:S(2)}, u32[]{:S(2)}) %collective-permute-start.2) | collective-permute-done | bytes 655392 | tf_op jit(solution)/shard_map/ppermute | solution.py:216
  24.1 0.1 slice_add_fusion.1
  24.2 0.3 collective-permute-start.3
  24.5 4.1 %collective-permute-done.5 = f32[8,24,512]{2,1,0:T(8,128)S(1)} collective-permute-done((f32[8,24,512]{2,1,0:T(8,128)S(1)}, f32[8,24,512]{2,1,0:T(8,128)S(1)}, u32[]{:S(2)}, u32[]{:S(2)}) %collective-permute-start.5) | collective-permute-done | bytes 393248 | tf_op jit(solution)/shard_map/ppermute | solution.py:216
  28.7 0.3 collective-permute-start.7
  28.9 2.4 %collective-permute-done.3 = f32[4,40,512]{2,1,0:T(8,128)S(1)} collective-permute-done((f32[4,40,512]{2,1,0:T(8,128)S(1)}, f32[4,40,512]{2,1,0:T(8,128)S(1)}, u32[]{:S(2)}, u32[]{:S(2)}) %collective-permute-start.3) | collective-permute-done | bytes 327712 | tf_op jit(solution)/shard_map/ppermute | solution.py:216
  31.3 0.1 slice_add_fusion.5
  31.4 1.6 %collective-permute-start.6 = (f32[2,40,512]{2,1,0:T(8,128)S(1)}, f32[2,40,512]{2,1,0:T(8,128)S(1)}, u32[]{:S(2)}, u32[]{:S(2)}) collective-permute-start(f32[2,40,512]{2,1,0:T(8,128)S(1)} %slice_add_fusion.5), channel_id=1, source_target_pairs={{0,1},{1,0},{2,3},{3,2},{4,5},{5,4},{6,7},{7,6},{8,9},{9,8},{10,11... | collective-permute-start | bytes 491528 | tf_op jit(solution)/shard_map/ppermute | solution.py:216
  33.0 3.9 %collective-permute-done.7 = f32[4,24,512]{2,1,0:T(8,128)S(1)} collective-permute-done((f32[4,24,512]{2,1,0:T(8,128)S(1)}, f32[4,24,512]{2,1,0:T(8,128)S(1)}, u32[]{:S(2)}, u32[]{:S(2)}) %collective-permute-start.7) | collective-permute-done | bytes 196640 | tf_op jit(solution)/shard_map/ppermute | solution.py:216
  37.0 0.1 collective-permute-start.9
  37.1 1.6 %collective-permute-done.6 = f32[2,40,512]{2,1,0:T(8,128)S(1)} collective-permute-done((f32[2,40,512]{2,1,0:T(8,128)S(1)}, f32[2,40,512]{2,1,0:T(8,128)S(1)}, u32[]{:S(2)}, u32[]{:S(2)}) %collective-permute-start.6) | collective-permute-done | bytes 163872 | tf_op jit(solution)/shard_map/ppermute | solution.py:216
  38.7 0.1 slice_add_fusion.11
  38.8 1.0 %collective-permute-start.8 = (f32[1,40,512]{2,1,0:T(8,128)S(1)}, f32[1,40,512]{2,1,0:T(8,128)S(1)}, u32[]{:S(2)}, u32[]{:S(2)}) collective-permute-start(f32[1,40,512]{2,1,0:T(8,128)S(1)} %get-tuple-element.26), channel_id=1, source_target_pairs={{0,2},{1,3},{2,0},{3,1},{4,6},{5,7},{6,4},{7,5},{8,10},{9,11},{10,... | collective-permute-start | bytes 245768 | tf_op jit(solution)/shard_map/ppermute | solution.py:216
  39.8 1.9 %collective-permute-done.9 = f32[2,24,512]{2,1,0:T(8,128)S(1)} collective-permute-done((f32[2,24,512]{2,1,0:T(8,128)S(1)}, f32[2,24,512]{2,1,0:T(8,128)S(1)}, u32[]{:S(2)}, u32[]{:S(2)}) %collective-permute-start.9) | collective-permute-done | bytes 98336 | tf_op jit(solution)/shard_map/ppermute | solution.py:216
  41.7 0.5 collective-permute-start.10
  42.3 3.6 %collective-permute-done.10 = f32[1,24,512]{2,1,0:T(8,128)S(1)} collective-permute-done((f32[1,24,512]{2,1,0:T(8,128)S(1)}, f32[1,24,512]{2,1,0:T(8,128)S(1)}, u32[]{:S(2)}, u32[]{:S(2)}) %collective-permute-start.10) | collective-permute-done | bytes 49184 | tf_op jit(solution)/shard_map/ppermute | solution.py:216
  45.9 0.0 collective-permute-done.8
  45.9 0.0 copy-done
  45.9 0.5 stats.1
  46.4 10.6 %all_to_all.11 = f32[32,1,128]{2,1,0:T(1,128)S(1)} all-to-all(f32[32,1,128]{2,1,0:T(1,128)S(1)} %bitcast.32), channel_id=1, replica_groups=mesh['ops'=8,'sec'=4] {'ops','sec'}, dimensions={0} | all-to-all | bytes 32768 | tf_op jit(solution)/shard_map/all_to_all | solution.py:274
  57.0 1.3 %finish.1 = (f32[1,64,512]{2,1,0:T(8,128)}, f32[1,64,512]{2,1,0:T(8,128)}, f32[2]{0:T(128)}) custom-call(f32[64,512]{1,0:T(8,128)S(1)} %get-tuple-element.28.psi_ref, f32[64,512]{1,0:T(8,128)S(1)} %get-tuple-element.29.held_ref, f32[32,128]{1,0:T(8,128)S(1)} %bitcast.30), custom_call_target="tpu_custom_call" | custom-call | tf_op jit(solution)/shard_map/finish/pallas_call | solution.py:275
  (4 shorter events, 0.1 us)
Async XLA Ops:
  6.4 2.9 %collective-permute-start.1 = (f32[8,40,512]{2,1,0:T(8,128)S(1)}, f32[8,40,512]{2,1,0:T(8,128)S(1)}, u32[]{:S(2)}, u32[]{:S(2)}) collective-permute-start(f32[8,40,512]{2,1,0:T(8,128)S(1)} %get-tuple-element.20), channel_id=1, source_target_pairs={{0,4},{4,0},{8,12},{12,8},{16,20},{20,16},{24,28},{28,24},{1,5},{5... | collective-permute-start | bytes 1966088 | tf_op jit(solution)/shard_map/ppermute | solution.py:243
  7.6 8.0 %collective-permute-start.4 = (f32[16,24,512]{2,1,0:T(8,128)S(1)}, f32[16,24,512]{2,1,0:T(8,128)S(1)}, u32[]{:S(2)}, u32[]{:S(2)}) collective-permute-start(f32[16,24,512]{2,1,0:T(8,128)S(1)} %get-tuple-element.22), channel_id=1, source_target_pairs={{0,4},{4,0},{8,12},{12,8},{16,20},{20,16},{24,28},{28,24},{1,5},{5... | collective-permute-start | bytes 2359304 | tf_op jit(solution)/shard_map/ppermute | solution.py:243
  7.7 10.1 %collective-permute-start = (f32[8,40,512]{2,1,0:T(8,128)S(1)}, f32[8,40,512]{2,1,0:T(8,128)S(1)}, u32[]{:S(2)}, u32[]{:S(2)}) collective-permute-start(f32[8,40,512]{2,1,0:T(8,128)S(1)} %get-tuple-element.18), channel_id=1, source_target_pairs={{0,4},{4,0},{8,12},{12,8},{16,20},{20,16},{24,28},{28,24},{1,5},{5... | collective-permute-start | bytes 1966088 | tf_op jit(solution)/shard_map/ppermute | solution.py:243
  9.3 36.6 %copy-start = (f32[1,512,512]{2,1,0:T(8,128)S(1)}, f32[1,512,512]{2,1,0:T(8,128)}, u32[]{:S(2)}) copy-start(f32[1,512,512]{2,1,0:T(8,128)} %psi_ref.3) | copy-start | bytes 3145732
  9.4 14.7 %collective-permute-start.2 = (f32[8,40,512]{2,1,0:T(8,128)S(1)}, f32[8,40,512]{2,1,0:T(8,128)S(1)}, u32[]{:S(2)}, u32[]{:S(2)}) collective-permute-start(f32[8,40,512]{2,1,0:T(8,128)S(1)} %add.60), channel_id=1, source_target_pairs={{0,8},{1,9},{2,10},{3,11},{4,20},{5,21},{6,22},{7,23},{8,0},{9,1},... | collective-permute-start | bytes 1966088 | tf_op jit(solution)/shard_map/ppermute | solution.py:216
  15.6 13.0 %collective-permute-start.5 = (f32[8,24,512]{2,1,0:T(8,128)S(1)}, f32[8,24,512]{2,1,0:T(8,128)S(1)}, u32[]{:S(2)}, u32[]{:S(2)}) collective-permute-start(f32[8,24,512]{2,1,0:T(8,128)S(1)} %slice_add_fusion), channel_id=1, source_target_pairs={{0,2},{1,3},{2,0},{3,1},{4,5},{5,4},{6,7},{7,6},{8,10},{9,11},{10,... | collective-permute-start | bytes 1179656 | tf_op jit(solution)/shard_map/ppermute | solution.py:216
  24.2 7.1 %collective-permute-start.3 = (f32[4,40,512]{2,1,0:T(8,128)S(1)}, f32[4,40,512]{2,1,0:T(8,128)S(1)}, u32[]{:S(2)}, u32[]{:S(2)}) collective-permute-start(f32[4,40,512]{2,1,0:T(8,128)S(1)} %slice_add_fusion.1), channel_id=1, source_target_pairs={{0,16},{1,17},{2,18},{3,19},{4,12},{5,13},{6,14},{7,15},{8,24},{9,... | collective-permute-start | bytes 983048 | tf_op jit(solution)/shard_map/ppermute | solution.py:216
  28.7 8.3 %collective-permute-start.7 = (f32[4,24,512]{2,1,0:T(8,128)S(1)}, f32[4,24,512]{2,1,0:T(8,128)S(1)}, u32[]{:S(2)}, u32[]{:S(2)}) collective-permute-start(f32[4,24,512]{2,1,0:T(8,128)S(1)} %slice_add_fusion.3), channel_id=1, source_target_pairs={{0,1},{1,0},{2,3},{3,2},{4,6},{5,7},{6,4},{7,5},{8,9},{9,8},{10,11... | collective-permute-start | bytes 589832 | tf_op jit(solution)/shard_map/ppermute | solution.py:216
  31.4 7.3 %collective-permute-start.6 = (f32[2,40,512]{2,1,0:T(8,128)S(1)}, f32[2,40,512]{2,1,0:T(8,128)S(1)}, u32[]{:S(2)}, u32[]{:S(2)}) collective-permute-start(f32[2,40,512]{2,1,0:T(8,128)S(1)} %slice_add_fusion.5), channel_id=1, source_target_pairs={{0,1},{1,0},{2,3},{3,2},{4,5},{5,4},{6,7},{7,6},{8,9},{9,8},{10,11... | collective-permute-start | bytes 491528 | tf_op jit(solution)/shard_map/ppermute | solution.py:216
  37.0 4.7 %collective-permute-start.9 = (f32[2,24,512]{2,1,0:T(8,128)S(1)}, f32[2,24,512]{2,1,0:T(8,128)S(1)}, u32[]{:S(2)}, u32[]{:S(2)}) collective-permute-start(f32[2,24,512]{2,1,0:T(8,128)S(1)} %slice_add_fusion.8), channel_id=1, source_target_pairs={{0,8},{1,9},{2,10},{3,11},{4,12},{5,13},{6,14},{7,15},{8,0},{9,1},... | collective-permute-start | bytes 294920 | tf_op jit(solution)/shard_map/ppermute | solution.py:216
  38.8 7.1 %collective-permute-start.8 = (f32[1,40,512]{2,1,0:T(8,128)S(1)}, f32[1,40,512]{2,1,0:T(8,128)S(1)}, u32[]{:S(2)}, u32[]{:S(2)}) collective-permute-start(f32[1,40,512]{2,1,0:T(8,128)S(1)} %get-tuple-element.26), channel_id=1, source_target_pairs={{0,2},{1,3},{2,0},{3,1},{4,6},{5,7},{6,4},{7,5},{8,10},{9,11},{10,... | collective-permute-start | bytes 245768 | tf_op jit(solution)/shard_map/ppermute | solution.py:216
  41.7 4.2 %collective-permute-start.10 = (f32[1,24,512]{2,1,0:T(8,128)S(1)}, f32[1,24,512]{2,1,0:T(8,128)S(1)}, u32[]{:S(2)}, u32[]{:S(2)}) collective-permute-start(f32[1,24,512]{2,1,0:T(8,128)S(1)} %get-tuple-element.27), channel_id=1, source_target_pairs={{0,16},{1,17},{2,18},{3,19},{4,20},{5,21},{6,22},{7,23},{8,24},{9,... | collective-permute-start | bytes 147464 | tf_op jit(solution)/shard_map/ppermute | solution.py:216
